TPU v7x, 256 devices: a whole 4x4x8 slice. The times are simulated.
256 devices in a mesh: lon: 16 (over x_hi, y, core), lev: 16 (over x_lo, z).
Axes of the slice: x: 4 (x_hi: 2, x_lo: 2; x = x_hi * 2 + x_lo), y: 4, z: 8, core: 2. Of those that a mesh axis runs over, the one named last changes fastest.
Arguments:
- inputs: bfloat16 [128, 512, 1024], P('lev', 'lon'), may hold values from -36 to 36
- norm_gain: float32 [1024], replicated, may hold values from 0.25 to 1.75
- w_qkv: bfloat16 [1024, 3072], replicated, may hold values from -0.1875 to 0.1875
- w_out: bfloat16 [1024, 1024], replicated, may hold values from -0.1875 to 0.1875
- d_out: bfloat16 [128, 512, 1024], P('lev', 'lon'), may hold values from -6 to 6
- corner: int32 [128, 512], P('lev', 'lon'), may hold values from 0 to 4
Outputs:
- mixed_out: bfloat16 [128, 512, 1024], P('lev', 'lon')
- grad_input: bfloat16 [128, 512, 1024], P('lev', 'lon')
Inputs may be any that keep to these rules, and one draw needn't show every extreme that they name: 0 keeps a cell's whole window; 1 to 4 name the 3 x 3 corner block of offsets that is left out.
All inputs are finite; a program needn't handle non-finite values.
Results may differ from a plain program's by a relative error of at most 0.015.
Values may be sent and summed in bfloat16 or wider, within the bound.
A program may use at most 128 MiB of HBM per device.

v0:
```python
import jax
import jax.numpy as jnp
from jax import lax
from jax.sharding import PartitionSpec as P

HEADS = 16
RADIUS = 3


EPSILON = 1e-06
BAND_ROWS = 2


def passed_along(value, axis, steps):
    count = lax.axis_size(axis)
    leading, last = (max(0, -steps), min(count, count - steps))
    return lax.ppermute(value, axis, [(source, source + steps) for source in range(leading, last)])


def from_behind(array, axis, by):
    devices = lax.axis_size(axis)
    return lax.ppermute(array, axis, [(i, (i + by) % devices) for i in range(devices)])


def padded(array, sides, width):
    for axis, dim in sides:
        devices, length = (lax.axis_size(axis), array.shape[dim])
        up = [(i, (i + 1) % devices) for i in range(devices)]
        down = [(j, i) for i, j in up]
        last = lax.slice_in_dim(array, length - width, length, axis=dim)
        leading = lax.slice_in_dim(array, 0, width, axis=dim)
        before = lax.ppermute(last, axis, up)
        after = lax.ppermute(leading, axis, down)
        array = jnp.concatenate([before, array, after], axis=dim)
    return array


def pair_keep(near_row, near_col, codes, query_row, total_rows):
    inside = (jnp.abs(near_row) <= RADIUS) & (jnp.abs(near_col) <= RADIUS)
    target = query_row + near_row
    rows_fine = (query_row >= 0) & (query_row < total_rows) & (target >= 0) & (target < total_rows)
    dropped = (
        (codes == 1) & (near_row < 0) & (near_col < 0)
        | (codes == 2) & (near_row < 0) & (near_col > 0)
        | (codes == 3) & (near_row > 0) & (near_col < 0)
        | (codes == 4) & (near_row > 0) & (near_col > 0)
    )
    return inside & rows_fine & jnp.logical_not(dropped)


def return_rims(grad_ext, rows, cols):
    middle = grad_ext[RADIUS : RADIUS + rows]
    for direction in (1, -1):
        piece = grad_ext[RADIUS + rows :] if direction == 1 else grad_ext[:RADIUS]
        arrived = passed_along(piece.astype(jnp.bfloat16), "lev", direction).astype(piece.dtype)
        if direction == 1:
            middle = middle.at[:RADIUS].add(arrived)
        else:
            middle = middle.at[rows - RADIUS :].add(arrived)
    for direction in (1, -1):
        piece = middle[:, RADIUS + cols :] if direction == 1 else middle[:, :RADIUS]
        arrived = from_behind(piece.astype(jnp.bfloat16), "lon", direction).astype(piece.dtype)
        if direction == 1:
            middle = middle.at[:, RADIUS : 2 * RADIUS].add(arrived)
        else:
            middle = middle.at[:, cols : cols + RADIUS].add(arrived)
    return middle[:, RADIUS : RADIUS + cols]


def shards(inputs, norm_gain, w_qkv, w_out, d_out, corner):
    rows, cols, width = inputs.shape
    head_dim = width // HEADS
    score_scale = head_dim ** (-0.5)
    first_row = lax.axis_index("lev") * rows
    total_rows = rows * lax.axis_size("lev")
    ext_rows = rows + 2 * RADIUS
    ext_cols = cols + 2 * RADIUS
    span_rows = BAND_ROWS + 2 * RADIUS
    band_cells = BAND_ROWS * cols
    span_cells = span_rows * ext_cols
    band_count = rows // BAND_ROWS
    contract_rows = (((1,), (1,)), ((), ()))
    inputs_f = inputs.astype(jnp.float32)
    inv_rms = lax.rsqrt(jnp.mean(inputs_f * inputs_f, axis=-1, keepdims=True) + EPSILON)
    normed = (inputs_f * inv_rms * norm_gain).astype(jnp.bfloat16)
    flat = normed.reshape(rows * cols, width)
    query = jnp.dot(flat, w_qkv[:, :width], preferred_element_type=jnp.float32).astype(jnp.bfloat16)
    pair_own = jnp.dot(flat, w_qkv[:, width:], preferred_element_type=jnp.float32).astype(
        jnp.bfloat16
    )
    pair_ext = padded(pair_own.reshape(rows, cols, 2 * width), (("lon", 1), ("lev", 0)), RADIUS)
    pair_ext = pair_ext.reshape(ext_rows, ext_cols, 2, HEADS, head_dim)
    key_ext = pair_ext[:, :, 0]
    value_ext = pair_ext[:, :, 1]
    query_heads = query.reshape(rows, cols, HEADS, head_dim)
    d_attn = lax.dot_general(
        d_out.reshape(rows * cols, width), w_out, contract_rows, preferred_element_type=jnp.float32
    ).astype(jnp.bfloat16)
    d_attn_heads = d_attn.reshape(rows, cols, HEADS, head_dim)
    band_index = jnp.arange(band_cells)
    span_index = jnp.arange(span_cells)
    band_row = (band_index // cols)[:, None]
    band_col = (band_index % cols)[:, None]
    span_row = (span_index // ext_cols)[None, :]
    span_col = (span_index % ext_cols)[None, :]
    fwd_near_row = span_row - RADIUS - band_row
    fwd_near_col = span_col - RADIUS - band_col
    grad_init = jnp.zeros((ext_rows, ext_cols, 2 * width), jnp.float32)
    carry_init = (
        jnp.zeros((rows, cols, HEADS, head_dim), jnp.bfloat16),
        jnp.zeros((rows, cols, HEADS, head_dim), jnp.bfloat16),
        jnp.zeros((HEADS, rows, cols), jnp.float32),
        jnp.zeros((HEADS, rows, cols), jnp.float32),
        grad_init,
    )

    def forward_band(band, carry):
        attended_all, gquery_all, denom_all, delta_all, grad_ext = carry
        start = band * BAND_ROWS
        q_band = lax.dynamic_slice_in_dim(query_heads, start, BAND_ROWS, 0).reshape(
            band_cells, HEADS, head_dim
        )
        g_band = lax.dynamic_slice_in_dim(d_attn_heads, start, BAND_ROWS, 0).reshape(
            band_cells, HEADS, head_dim
        )
        k_band = lax.dynamic_slice_in_dim(key_ext, start, span_rows, 0).reshape(
            span_cells, HEADS, head_dim
        )
        v_band = lax.dynamic_slice_in_dim(value_ext, start, span_rows, 0).reshape(
            span_cells, HEADS, head_dim
        )
        codes = lax.dynamic_slice_in_dim(corner, start, BAND_ROWS, 0).reshape(band_cells)[:, None]
        keep_now = pair_keep(
            fwd_near_row, fwd_near_col, codes, first_row + start + band_row, total_rows
        )
        scores = (
            jnp.einsum("qhd,khd->hqk", q_band, k_band, preferred_element_type=jnp.float32)
            * score_scale
        )
        exp_terms = jnp.where(keep_now[None], jnp.exp(scores), 0.0)
        denominator = jnp.sum(exp_terms, axis=-1)
        weights_f = exp_terms / denominator[:, :, None]
        weights_b = weights_f.astype(jnp.bfloat16)
        attended = jnp.einsum("hqk,khd->qhd", weights_b, v_band, preferred_element_type=jnp.float32)
        grad_prob = jnp.einsum("qhd,khd->hqk", g_band, v_band, preferred_element_type=jnp.float32)
        row_delta = jnp.sum(weights_f * grad_prob, axis=-1)
        dscore_b = (weights_f * (grad_prob - row_delta[:, :, None])).astype(jnp.bfloat16)
        grad_query = jnp.einsum(
            "hqk,khd->qhd", dscore_b, k_band, preferred_element_type=jnp.float32
        )
        attended_all = lax.dynamic_update_slice(
            attended_all,
            attended.astype(jnp.bfloat16).reshape(BAND_ROWS, cols, HEADS, head_dim),
            (start, 0, 0, 0),
        )
        gquery_all = lax.dynamic_update_slice(
            gquery_all,
            (grad_query * score_scale)
            .astype(jnp.bfloat16)
            .reshape(BAND_ROWS, cols, HEADS, head_dim),
            (start, 0, 0, 0),
        )
        denom_all = lax.dynamic_update_slice(
            denom_all, denominator.reshape(HEADS, BAND_ROWS, cols), (0, start, 0)
        )
        delta_all = lax.dynamic_update_slice(
            delta_all, row_delta.reshape(HEADS, BAND_ROWS, cols), (0, start, 0)
        )
        grad_key = jnp.einsum("hqk,qhd->khd", dscore_b, q_band, preferred_element_type=jnp.float32)
        grad_value = jnp.einsum(
            "hqk,qhd->khd", weights_b, g_band, preferred_element_type=jnp.float32
        )
        addition = jnp.concatenate(
            [
                grad_key.reshape(span_rows, ext_cols, width),
                grad_value.reshape(span_rows, ext_cols, width),
            ],
            axis=-1,
        )
        current = lax.dynamic_slice_in_dim(grad_ext, start, span_rows, 0)
        grad_ext = lax.dynamic_update_slice(grad_ext, current + addition, (start, 0, 0))
        return (attended_all, gquery_all, denom_all, delta_all, grad_ext)

    attended_all, gquery_all, denom_all, delta_all, grad_ext = lax.fori_loop(
        0, band_count, forward_band, carry_init
    )
    grad_ext = jnp.concatenate(
        [grad_ext[:, :, :width] * score_scale, grad_ext[:, :, width:]], axis=-1
    )
    grad_own = return_rims(grad_ext, rows, cols)
    grad_key = grad_own[:, :, :width]
    grad_value = grad_own[:, :, width:]
    grad_qkv = jnp.concatenate(
        [
            gquery_all.reshape(rows * cols, width),
            grad_key.astype(jnp.bfloat16).reshape(rows * cols, width),
            grad_value.astype(jnp.bfloat16).reshape(rows * cols, width),
        ],
        axis=1,
    )
    d_normed = lax.dot_general(grad_qkv, w_qkv, contract_rows, preferred_element_type=jnp.float32)
    scaled = d_normed.reshape(rows, cols, width) * norm_gain
    grad_input = inv_rms * scaled - inputs_f * inv_rms**3 * jnp.mean(
        inputs_f * scaled, axis=-1, keepdims=True
    )
    mixed_out = jnp.dot(
        attended_all.reshape(rows * cols, width), w_out, preferred_element_type=jnp.float32
    ).astype(jnp.bfloat16)
    return (mixed_out.reshape(rows, cols, width), grad_input.astype(jnp.bfloat16))


def solution(mesh):
    placed = (P("lev", "lon", None), P(), P(), P(), P("lev", "lon", None), P("lev", "lon"))
    return jax.shard_map(
        shards,
        mesh=mesh,
        in_specs=placed,
        out_specs=(P("lev", "lon", None), P("lev", "lon", None)),
        check_vma=False,
    )
```

profile of v0, /device:TPU:2, one launch (start us, length us, event | category | flops | bytes accessed | tf_op | source)
XLA Modules:
  0.0 313.3 jit_solution(11606065495015663885)
XLA Ops:
  3.3 3.4 %fusion.46 = bf16[256,2048]{1,0:T(8,128)(2,1)S(1)} fusion(bf16[256,1024]{1,0:T(8,128)(2,1)S(1)} %bitcast.124, bf16[1024,3072]{1,0:T(8,128)(2,1)} %param.18), kind=kOutput, calls=%fused_computation.77 | convolution fusion | flops 1074266112 | bytes 5767168 | tf_op jit(solution)/shard_map/dot_general | solution.py:88
  7.5 5.4 %collective-permute-start.1 = (bf16[8,3,2048]{2,1,0:T(4,128)(2,1)S(1)}, bf16[8,3,2048]{2,1,0:T(4,128)(2,1)S(1)}, u32[]{:S(2)}, u32[]{:S(2)}) collective-permute-start(bf16[8,3,2048]{2,1,0:T(4,128)(2,1)S(1)} %get-tuple-element.574), channel_id=1, source_target_pairs={{16,0},{32,16},{48,32},{64,48},{80,64},{96,80},{112,96},{128,112},... | collective-permute-start | bytes 294920 | tf_op jit(solution)/shard_map/ppermute | solution.py:33
  12.9 3.1 fusion.57
  21.7 3.9 %collective-permute-start.3 = (bf16[3,38,2048]{2,1,0:T(8,128)(2,1)}, bf16[3,38,2048]{2,1,0:T(8,128)(2,1)}, u32[]{:S(2)}, u32[]{:S(2)}) collective-permute-start(bf16[3,38,2048]{2,1,0:T(8,128)(2,1)} %get-tuple-element.572), channel_id=1, source_target_pairs={{1,0},{2,1},{3,2},{4,3},{5,4},{6,5},{7,6},{8,7},{9,8},{10,9},{11,1... | collective-permute-start | bytes 1400840 | tf_op jit(solution)/shard_map/ppermute | solution.py:33
  29.6 4.0 %collective-permute-done.2 = bf16[3,38,2048]{2,1,0:T(8,128)(2,1)} collective-permute-done((bf16[3,38,2048]{2,1,0:T(8,128)(2,1)}, bf16[3,38,2048]{2,1,0:T(8,128)(2,1)}, u32[]{:S(2)}, u32[]{:S(2)}) %collective-permute-start.2) | collective-permute-done | bytes 466976 | tf_op jit(solution)/shard_map/ppermute | solution.py:32
  33.6 2.8 pad_maximum_fusion.1
  36.5 6.9 %reshape.576 = bf16[14,38,2,16,64]{4,3,2,1,0:T(8,128)(2,1)} reshape(bf16[14,38,2048]{2,1,0:T(8,128)(2,1)} %pad_maximum_fusion.1) | data formatting | bytes 4358144 | tf_op jit(solution)/shard_map/reshape | solution.py:92
  43.4 5.2 %slice_bitcast_fusion = (bf16[14,38,16,64]{3,2,1,0:T(8,128)(2,1)}, bf16[14,38,16,64]{3,2,1,0:T(8,128)(2,1)}) fusion(bf16[14,38,2,16,64]{4,3,2,1,0:T(8,128)(2,1)} %reshape.576), kind=kLoop, calls=%fused_computation.80 | loop fusion | bytes 4358144 | tf_op jit(solution)/shard_map/squeeze | solution.py:93
  50.8 2.7 broadcast_in_dim.49
  53.4 206.2 %while.25 = (s32[]{:T(128)}, bf16[8,32,16,64]{3,2,1,0:T(8,128)(2,1)}, bf16[8,32,16,64]{3,2,1,0:T(8,128)(2,1)}, f32[14,38,2048]{2,1,0:T(8,128)}, bf16[14,38,16,64...) while((s32[]{:T(128)}, ...), condition=%wide.region_4.5_spmd.clone.clone.clone, body=%wide.region_1.4_spmd.clone.clone.clone.sunk | while | flops 244879824 | bytes 51727452 | solution.py:184
  56.8 2.6 constant_dynamic-slice_fusion.9
  61.3 2.6 constant_dynamic-slice_fusion.11
  63.9 2.5 copy.51
  67.9 3.4 %fusion.146 = bf16[64,16,64]{0,2,1:T(8,128)(2,1)} fusion(bf16[304,16,64]{0,2,1:T(8,128)(2,1)} %copy.51, f32[16,64,304]{2,1,0:T(8,128)} %exponential_select_fusion.2), kind=kOutput, calls=%fused_computation.15.clone.1 | convolution fusion | flops 40535344 | bytes 1998848 | tf_op jit(solution)/shard_map/while/body/eval_jaxpr/hqk,khd->qhd/dot_general | solution.py:144
  73.2 2.6 fusion.142
  75.9 3.8 %convolution_bitcast_fusion.4 = f32[304,16,64]{0,2,1:T(8,128)} fusion(bf16[64,16,64]{2,0,1:T(8,128)(2,1)S(1)} %bitcast.117, f32[16,64,304]{2,1,0:T(8,128)} %exponential_select_fusion.2), kind=kOutput, calls=%fused_computation.10.clone.1 | convolution fusion | flops 40469808 | bytes 2621440 | tf_op jit(solution)/shard_map/while/body/eval_jaxpr/hqk,qhd->khd/dot_general | solution.py:170
  79.7 2.8 multiply_reduce_fusion.2
  85.0 2.7 convolution_bitcast_fusion.5
  87.7 3.1 copy.56
  93.0 3.1 copy.55
  96.1 3.0 reshape.612
  100.9 4.1 %fusion.147 = f32[14,38,2048]{2,1,0:T(8,128)} fusion(f32[14,38,2048]{2,1,0:T(8,128)} %get-tuple-element.704, s32[]{:T(128)S(6)} %select_n.156, f32[8,38,1024]{2,1,0:T(8,128)} %reshape.612, f32[8,38,1024]{2,1,0:T(8,128)S(1)} %reshape.613), kind=kLoop, calls=%fused_computation.6.clone.1 | loop fusion | flops 1245184 | bytes 7798788 | tf_op jit(solution)/shard_map/while/body/eval_jaxpr/dynamic_update_slice | solution.py:181
  108.4 2.6 constant_dynamic-slice_fusion.9
  112.9 2.6 constant_dynamic-slice_fusion.11
  115.5 2.5 copy.51
  119.5 3.4 %fusion.146 = bf16[64,16,64]{0,2,1:T(8,128)(2,1)} fusion(bf16[304,16,64]{0,2,1:T(8,128)(2,1)} %copy.51, f32[16,64,304]{2,1,0:T(8,128)} %exponential_select_fusion.2), kind=kOutput, calls=%fused_computation.15.clone.1 | convolution fusion | flops 40535344 | bytes 1998848 | tf_op jit(solution)/shard_map/while/body/eval_jaxpr/hqk,khd->qhd/dot_general | solution.py:144
  124.8 2.6 fusion.142
  127.5 3.8 %convolution_bitcast_fusion.4 = f32[304,16,64]{0,2,1:T(8,128)} fusion(bf16[64,16,64]{2,0,1:T(8,128)(2,1)S(1)} %bitcast.117, f32[16,64,304]{2,1,0:T(8,128)} %exponential_select_fusion.2), kind=kOutput, calls=%fused_computation.10.clone.1 | convolution fusion | flops 40469808 | bytes 2621440 | tf_op jit(solution)/shard_map/while/body/eval_jaxpr/hqk,qhd->khd/dot_general | solution.py:170
  131.3 2.8 multiply_reduce_fusion.2
  136.6 2.7 convolution_bitcast_fusion.5
  139.3 3.1 copy.56
  144.6 3.1 copy.55
  147.7 3.0 reshape.612
  152.5 4.1 %fusion.147 = f32[14,38,2048]{2,1,0:T(8,128)} fusion(f32[14,38,2048]{2,1,0:T(8,128)} %get-tuple-element.704, s32[]{:T(128)S(6)} %select_n.156, f32[8,38,1024]{2,1,0:T(8,128)} %reshape.612, f32[8,38,1024]{2,1,0:T(8,128)S(1)} %reshape.613), kind=kLoop, calls=%fused_computation.6.clone.1 | loop fusion | flops 1245184 | bytes 7798788 | tf_op jit(solution)/shard_map/while/body/eval_jaxpr/dynamic_update_slice | solution.py:181
  160.0 2.6 constant_dynamic-slice_fusion.9
  164.4 2.6 constant_dynamic-slice_fusion.11
  171.1 3.4 %fusion.146 = bf16[64,16,64]{0,2,1:T(8,128)(2,1)} fusion(bf16[304,16,64]{0,2,1:T(8,128)(2,1)} %copy.51, f32[16,64,304]{2,1,0:T(8,128)} %exponential_select_fusion.2), kind=kOutput, calls=%fused_computation.15.clone.1 | convolution fusion | flops 40535344 | bytes 1998848 | tf_op jit(solution)/shard_map/while/body/eval_jaxpr/hqk,khd->qhd/dot_general | solution.py:144
  176.4 2.6 fusion.142
  179.0 3.8 %convolution_bitcast_fusion.4 = f32[304,16,64]{0,2,1:T(8,128)} fusion(bf16[64,16,64]{2,0,1:T(8,128)(2,1)S(1)} %bitcast.117, f32[16,64,304]{2,1,0:T(8,128)} %exponential_select_fusion.2), kind=kOutput, calls=%fused_computation.10.clone.1 | convolution fusion | flops 40469808 | bytes 2621440 | tf_op jit(solution)/shard_map/while/body/eval_jaxpr/hqk,qhd->khd/dot_general | solution.py:170
  182.9 2.8 multiply_reduce_fusion.2
  188.2 2.7 convolution_bitcast_fusion.5
  190.9 3.1 copy.56
  196.2 3.1 copy.55
  199.2 3.0 reshape.612
  204.1 4.0 %fusion.147 = f32[14,38,2048]{2,1,0:T(8,128)} fusion(f32[14,38,2048]{2,1,0:T(8,128)} %get-tuple-element.704, s32[]{:T(128)S(6)} %select_n.156, f32[8,38,1024]{2,1,0:T(8,128)} %reshape.612, f32[8,38,1024]{2,1,0:T(8,128)S(1)} %reshape.613), kind=kLoop, calls=%fused_computation.6.clone.1 | loop fusion | flops 1245184 | bytes 7798788 | tf_op jit(solution)/shard_map/while/body/eval_jaxpr/dynamic_update_slice | solution.py:181
  211.5 2.6 constant_dynamic-slice_fusion.9
  215.9 2.6 constant_dynamic-slice_fusion.11
  222.6 3.4 %fusion.146 = bf16[64,16,64]{0,2,1:T(8,128)(2,1)} fusion(bf16[304,16,64]{0,2,1:T(8,128)(2,1)} %copy.51, f32[16,64,304]{2,1,0:T(8,128)} %exponential_select_fusion.2), kind=kOutput, calls=%fused_computation.15.clone.1 | convolution fusion | flops 40535344 | bytes 1998848 | tf_op jit(solution)/shard_map/while/body/eval_jaxpr/hqk,khd->qhd/dot_general | solution.py:144
  227.9 2.6 fusion.142
  230.5 3.8 %convolution_bitcast_fusion.4 = f32[304,16,64]{0,2,1:T(8,128)} fusion(bf16[64,16,64]{2,0,1:T(8,128)(2,1)S(1)} %bitcast.117, f32[16,64,304]{2,1,0:T(8,128)} %exponential_select_fusion.2), kind=kOutput, calls=%fused_computation.10.clone.1 | convolution fusion | flops 40469808 | bytes 2621440 | tf_op jit(solution)/shard_map/while/body/eval_jaxpr/hqk,qhd->khd/dot_general | solution.py:170
  234.4 2.8 multiply_reduce_fusion.2
  239.7 2.7 convolution_bitcast_fusion.5
  242.4 3.1 copy.56
  247.7 3.1 copy.55
  250.8 3.0 reshape.612
  255.6 4.1 %fusion.147 = f32[14,38,2048]{2,1,0:T(8,128)} fusion(f32[14,38,2048]{2,1,0:T(8,128)} %get-tuple-element.704, s32[]{:T(128)S(6)} %select_n.156, f32[8,38,1024]{2,1,0:T(8,128)} %reshape.612, f32[8,38,1024]{2,1,0:T(8,128)S(1)} %reshape.613), kind=kLoop, calls=%fused_computation.6.clone.1 | loop fusion | flops 1245184 | bytes 7798788 | tf_op jit(solution)/shard_map/while/body/eval_jaxpr/dynamic_update_slice | solution.py:181
  259.7 2.8 fusion.81
  264.8 6.0 %collective-permute-start.5 = (bf16[3,38,2048]{2,1,0:T(8,128)(2,1)S(1)}, bf16[3,38,2048]{2,1,0:T(8,128)(2,1)S(1)}, u32[]{:S(2)}, u32[]{:S(2)}) collective-permute-start(bf16[3,38,2048]{2,1,0:T(8,128)(2,1)S(1)} %get-tuple-element.567), channel_id=1, source_target_pairs={{1,0},{2,1},{3,2},{4,3},{5,4},{6,5},{7,6},{8,7},{9,8},{10,9},{11,1... | collective-permute-start | bytes 1400840 | tf_op jit(solution)/shard_map/ppermute | solution.py:17
  271.0 4.7 %collective-permute-done.4 = bf16[3,38,2048]{2,1,0:T(8,128)(2,1)S(1)} collective-permute-done((bf16[3,38,2048]{2,1,0:T(8,128)(2,1)S(1)}, bf16[3,38,2048]{2,1,0:T(8,128)(2,1)S(1)}, u32[]{:S(2)}, u32[]{:S(2)}) %collective-permute-start.4) | collective-permute-done | bytes 466976 | tf_op jit(solution)/shard_map/ppermute | solution.py:17
  280.6 10.0 %collective-permute-done.6 = bf16[8,3,2048]{2,1,0:T(4,128)(2,1)S(1)} collective-permute-done((bf16[8,3,2048]{2,1,0:T(4,128)(2,1)S(1)}, bf16[8,3,2048]{2,1,0:T(4,128)(2,1)S(1)}, u32[]{:S(2)}, u32[]{:S(2)}) %collective-permute-start.6) | collective-permute-done | bytes 98336 | tf_op jit(solution)/shard_map/ppermute | solution.py:22
  291.7 3.7 %scatter-add.16 = f32[8,38,2048]{2,1,0:T(8,128)} dynamic-update-slice(f32[8,38,2048]{2,1,0:T(8,128)} %copy-done.3, f32[8,3,2048]{2,1,0:T(4,128)S(1)} %slice_add_fusion.2, s32[]{:T(128)} %constant.247.clone.1, s32[]{:T(128)} %constant.262.clone.1, s32[]{:T(128)} %constant.247.clone.1) | dynamic-update-slice | bytes 393220 | tf_op jit(solution)/shard_map/scatter-add | solution.py:64
  296.8 2.5 convolution_convert_fusion.1
  301.9 2.9 scatter-add.19
  307.3 4.7 %fusion.51 = f32[256,1024]{1,0:T(8,128)S(1)} fusion(bf16[1024,3072]{1,0:T(8,128)(2,1)} %param.18, bf16[256,1024]{1,0:T(8,128)(2,1)S(1)} %bitcast.127, bf16[256,1024]{1,0:T(8,128)(2,1)S(1)} %bitcast.126, bf16[256,1024]{1,0:T(8,128)(2,1)S(1)} %copy-done.7), kind=kOutput, calls=%fused_computation.88 | convolution fusion | flops 1615331328 | bytes 8912896 | tf_op jit(solution)/shard_map/dot_general | solution.py:201
  (152 shorter events, 97.1 us)
Async XLA Ops:
  0.6 25.0 %copy-start = (bf16[1024,1024]{1,0:T(8,128)(2,1)S(1)}, bf16[1024,1024]{1,0:T(8,128)(2,1)}, u32[]{:S(2)}) copy-start(bf16[1024,1024]{1,0:T(8,128)(2,1)} %param.19) | copy-start | bytes 6291460
  7.5 11.0 %collective-permute-start = (bf16[8,3,2048]{2,1,0:T(4,128)(2,1)}, bf16[8,3,2048]{2,1,0:T(4,128)(2,1)S(1)}, u32[]{:S(2)}, u32[]{:S(2)}) collective-permute-start(bf16[8,3,2048]{2,1,0:T(4,128)(2,1)} %get-tuple-element.573), channel_id=1, source_target_pairs={{0,16},{16,32},{32,48},{48,64},{64,80},{80,96},{96,112},{112,128},... | collective-permute-start | bytes 294920 | tf_op jit(solution)/shard_map/ppermute | solution.py:32
  7.5 11.0 %collective-permute-start.1 = (bf16[8,3,2048]{2,1,0:T(4,128)(2,1)S(1)}, bf16[8,3,2048]{2,1,0:T(4,128)(2,1)S(1)}, u32[]{:S(2)}, u32[]{:S(2)}) collective-permute-start(bf16[8,3,2048]{2,1,0:T(4,128)(2,1)S(1)} %get-tuple-element.574), channel_id=1, source_target_pairs={{16,0},{32,16},{48,32},{64,48},{80,64},{96,80},{112,96},{128,112},... | collective-permute-start | bytes 294920 | tf_op jit(solution)/shard_map/ppermute | solution.py:33
  18.5 7.1 %copy-start.9 = (bf16[8,32,1024]{2,1,0:T(8,128)(2,1)S(1)}, bf16[8,32,1024]{2,1,0:T(8,128)(2,1)}, u32[]{:S(2)}) copy-start(bf16[8,32,1024]{2,1,0:T(8,128)(2,1)} %param.20) | copy-start | bytes 1572868
  19.8 13.9 %collective-permute-start.2 = (bf16[3,38,2048]{2,1,0:T(8,128)(2,1)}, bf16[3,38,2048]{2,1,0:T(8,128)(2,1)}, u32[]{:S(2)}, u32[]{:S(2)}) collective-permute-start(bf16[3,38,2048]{2,1,0:T(8,128)(2,1)} %get-tuple-element.571), channel_id=1, source_target_pairs={{0,1},{1,2},{2,3},{3,4},{4,5},{5,6},{6,7},{7,8},{8,9},{9,10},{10,1... | collective-permute-start | bytes 1400840 | tf_op jit(solution)/shard_map/ppermute | solution.py:32
  21.7 11.9 %collective-permute-start.3 = (bf16[3,38,2048]{2,1,0:T(8,128)(2,1)}, bf16[3,38,2048]{2,1,0:T(8,128)(2,1)}, u32[]{:S(2)}, u32[]{:S(2)}) collective-permute-start(bf16[3,38,2048]{2,1,0:T(8,128)(2,1)} %get-tuple-element.572), channel_id=1, source_target_pairs={{1,0},{2,1},{3,2},{4,3},{5,4},{6,5},{7,6},{8,7},{9,8},{10,9},{11,1... | collective-permute-start | bytes 1400840 | tf_op jit(solution)/shard_map/ppermute | solution.py:33
  79.7 2.8 copy-start.2
  82.8 0.9 copy-start.1
  131.3 2.8 copy-start.2
  134.4 0.9 copy-start.1
  182.8 2.8 copy-start.2
  185.9 0.9 copy-start.1
  234.4 2.8 copy-start.2
  237.4 0.9 copy-start.1
  262.9 12.8 %collective-permute-start.4 = (bf16[3,38,2048]{2,1,0:T(8,128)(2,1)S(1)}, bf16[3,38,2048]{2,1,0:T(8,128)(2,1)S(1)}, u32[]{:S(2)}, u32[]{:S(2)}) collective-permute-start(bf16[3,38,2048]{2,1,0:T(8,128)(2,1)S(1)} %get-tuple-element.568), channel_id=1, source_target_pairs={{0,1},{1,2},{2,3},{3,4},{4,5},{5,6},{6,7},{7,8},{8,9},{9,10},{10,1... | collective-permute-start | bytes 1400840 | tf_op jit(solution)/shard_map/ppermute | solution.py:17
  264.8 12.4 %collective-permute-start.5 = (bf16[3,38,2048]{2,1,0:T(8,128)(2,1)S(1)}, bf16[3,38,2048]{2,1,0:T(8,128)(2,1)S(1)}, u32[]{:S(2)}, u32[]{:S(2)}) collective-permute-start(bf16[3,38,2048]{2,1,0:T(8,128)(2,1)S(1)} %get-tuple-element.567), channel_id=1, source_target_pairs={{1,0},{2,1},{3,2},{4,3},{5,4},{6,5},{7,6},{8,7},{9,8},{10,9},{11,1... | collective-permute-start | bytes 1400840 | tf_op jit(solution)/shard_map/ppermute | solution.py:17
  275.8 3.2 %copy-start.6 = (bf16[8,32,16,64]{3,2,1,0:T(8,128)(2,1)S(1)}, bf16[8,32,16,64]{3,2,1,0:T(8,128)(2,1)}, u32[]{:S(2)}) copy-start(bf16[8,32,16,64]{3,2,1,0:T(8,128)(2,1)} %get-tuple-element.348) | copy-start | bytes 1572868
  277.4 1.5 copy-start.3
  279.0 11.6 %collective-permute-start.6 = (bf16[8,3,2048]{2,1,0:T(4,128)(2,1)S(1)}, bf16[8,3,2048]{2,1,0:T(4,128)(2,1)S(1)}, u32[]{:S(2)}, u32[]{:S(2)}) collective-permute-start(bf16[8,3,2048]{2,1,0:T(4,128)(2,1)S(1)} %slice.230), channel_id=1, source_target_pairs={{0,16},{16,32},{32,48},{48,64},{64,80},{80,96},{96,112},{112,128},... | collective-permute-start | bytes 294920 | tf_op jit(solution)/shard_map/ppermute | solution.py:22
  291.7 7.6 %copy-start.5 = (bf16[8,32,16,64]{3,2,1,0:T(8,128)(2,1)S(1)}, bf16[8,32,16,64]{3,2,1,0:T(8,128)(2,1)}, u32[]{:S(2)}) copy-start(bf16[8,32,16,64]{3,2,1,0:T(8,128)(2,1)} %get-tuple-element.349) | copy-start | bytes 1572868
  296.5 4.4 %collective-permute-start.7 = (bf16[8,3,2048]{2,1,0:T(4,128)(2,1)S(1)}, bf16[8,3,2048]{2,1,0:T(4,128)(2,1)S(1)}, u32[]{:S(2)}, u32[]{:S(2)}) collective-permute-start(bf16[8,3,2048]{2,1,0:T(4,128)(2,1)S(1)} %slice.229), channel_id=1, source_target_pairs={{0,240},{16,0},{32,16},{48,32},{64,48},{80,64},{96,80},{112,96},{1... | collective-permute-start | bytes 294920 | tf_op jit(solution)/shard_map/ppermute | solution.py:22
  304.9 2.4 copy-start.7
  307.3 4.7 %copy-start.4 = (bf16[8,32,1024]{2,1,0:T(8,128)(2,1)S(1)}, bf16[8,32,1024]{2,1,0:T(8,128)(2,1)}, u32[]{:S(2)}) copy-start(bf16[8,32,1024]{2,1,0:T(8,128)(2,1)} %param.16) | copy-start | bytes 1572868
  307.3 4.7 %copy-start.8 = (f32[1024]{0:T(1024)S(1)}, f32[1024]{0:T(1024)}, u32[]{:S(2)}) copy-start(f32[1024]{0:T(1024)} %param.17) | copy-start | bytes 12292
where the time goes:
time: 317 us; the launch traced here: 313 us
  local copies, waits for them, and re-layouts  151 us (48%)
  matrix products  73.5 us (23%)
  other arithmetic  48.1 us (15%)
  waiting for transfers between devices  20 us (6%)
  starting transfers between devices  19.5 us (6%)
    dynamic_update_slice x4, other arithmetic, forward_band(): lax.dynamic_update_slice(grad_ext, current + addition, (start, 0, 0))  16.3 us
    dot_general x4, matrix products, forward_band(): jnp.einsum('hqk,qhd->khd', weights_b, g_band, preferred_element_type=jnp....  15.3 us
    dot_general x4, matrix products, forward_band(): jnp.einsum('hqk,khd->qhd', weights_b, v_band, preferred_element_type=jnp....  13.7 us
    transpose x4, local copies, waits for them, and re-layouts, forward_band(): jnp.einsum('hqk,qhd->khd', weights_b, g_band, preferred_element_type=jnp....  12.3 us
    transpose x4, local copies, waits for them, and re-layouts, forward_band(): jnp.einsum('hqk,qhd->khd', dscore_b, q_band, preferred_element_type=jnp.f...  12.3 us
    reshape x4, local copies, waits for them, and re-layouts, forward_band(): grad_value.reshape(span_rows, ext_cols, width)  12 us
    div x4, other arithmetic, forward_band(): weights_f = exp_terms / denominator[:, :, None]  11.3 us
    dot_general x4, matrix products, forward_band(): jnp.einsum('hqk,qhd->khd', dscore_b, q_band, preferred_element_type=jnp.f...  10.8 us
  transfers between devices with their start and end apart: 8, of which 4 were waited for; matrix products, arithmetic and copies ran while one was open for 5% of the time, Pallas kernels for 0%

commit v1 on v0

v1 whole, which is shorter than its diff:
```python
import jax
import jax.numpy as jnp
import numpy as np
from jax import lax
from jax.experimental import pallas as pl
from jax.experimental.pallas import tpu as pltpu
from jax.sharding import PartitionSpec as P

HEADS = 16
RADIUS = 3
EPSILON = 1e-06

ROWS, COLS, WIDTH = 8, 32, 1024
CELLS = ROWS * COLS
HEAD_DIM = WIDTH // HEADS
QUAD = 4 * HEAD_DIM
QUADS = WIDTH // QUAD
TILE = 8
TILES = COLS // TILE
EXT = ROWS + 2 * RADIUS
SPAN = EXT * 2 * TILE
RIM = RADIUS * COLS
EDGE = EXT * TILE
PACK = 128
HALO = 2 * RIM + PACK
NEG = -1e30

PIECES = (
    ((0, -1), 0, 32),
    ((0, 1), 32, 32),
    ((-1, -1), 64, 16),
    ((-1, 1), 80, 16),
    ((1, -1), 96, 16),
    ((1, 1), 112, 16),
)
AROUND = ((-1, 0), (1, 0)) + tuple(p[0] for p in PIECES)
OPPOSITE = tuple(AROUND.index((-d[0], -d[1])) for d in AROUND)


def selections():
    pack = np.zeros((PACK, CELLS), np.float32)
    spread = np.zeros((EDGE, PACK), np.float32)
    for (up, side), at, _ in PIECES:
        own_rows = {-1: range(RADIUS), 0: range(ROWS), 1: range(ROWS - RADIUS, ROWS)}[up]
        ext_row = {-1: 0, 0: RADIUS, 1: RADIUS + ROWS}[up]
        for i, row in enumerate(own_rows):
            for c in range(RADIUS):
                col = c if side < 0 else COLS - RADIUS + c
                pack[at + i * RADIUS + c, row * COLS + col] = 1
                position = TILE - RADIUS + c if side < 0 else c
                spread[(ext_row + i) * TILE + position, at + i * RADIUS + c] = 1
    return pack, spread


def dot(a, b, dims=((1,), (0,))):
    return lax.dot_general(a, b, (dims, ((), ())), preferred_element_type=jnp.float32)


ROWS_BY_ROWS = ((1,), (1,))
COLS_BY_COLS = ((0,), (0,))


def lanes(index, size=QUAD):
    return pl.ds(pl.multiple_of(index * size, size), size)


def kernel(
    x_hbm, do_hbm, gain_hbm, corner_hbm, wqkv_hbm, wout_hbm, pack_hbm, packt_hbm, spread_hbm,
    spreadt_hbm,
    mixed_hbm, gin_hbm,
    x_v, do_v, gain_v, corner_v, w_v, wo_v, pack_v, packt_v, spread_v, spreadt_v,
    xn_v, xh_v, inv_v, q_v, da_v, kvx_v, kt_v, mask_v, dk_v, dv_v,
    att_v, g_v, gh_v, dn_v, mixed_v, gin_v,
    edge1_v, rim1_r, edge1_r, send2_v, recv2_v,
    in_sem, w_sem, out_sem, send1_sem, recv1_sem, send2_sem, recv2_sem,
):
    f32, bf16 = jnp.float32, jnp.bfloat16
    lon, lev = lax.axis_index("lon"), lax.axis_index("lev")
    lons, levs = lax.axis_size("lon"), lax.axis_size("lev")
    target = [
        {"lon": lax.rem(lon + dx + lons, lons), "lev": lax.rem(lev + dy + levs, levs)}
        for dy, dx in AROUND
    ]

    small = [
        pltpu.make_async_copy(src, dst, in_sem.at[i])
        for i, (src, dst) in enumerate(
            [
                (x_hbm, x_v), (pack_hbm, pack_v), (corner_hbm, corner_v), (gain_hbm, gain_v),
                (do_hbm, do_v), (spread_hbm, spread_v), (spreadt_hbm, spreadt_v),
                (packt_hbm, packt_v),
            ]
        )
    ]
    for copy in small:
        copy.start()

    def weight(c):
        return pltpu.make_async_copy(wqkv_hbm.at[:, lanes(c)], w_v.at[:, lanes(c)], w_sem.at[c])

    out_weight = pltpu.make_async_copy(wout_hbm, wo_v, w_sem.at[3 * QUADS])
    for c in range(3 * QUADS):
        weight(c).start()
    out_weight.start()

    barrier = pltpu.get_barrier_semaphore()
    for device in target:
        pl.semaphore_signal(
            barrier, inc=1, device_id=device, device_id_type=pl.DeviceIdType.MESH
        )

    def remote(src, dst, d, send_sem, recv_sem):
        return pltpu.make_async_remote_copy(
            src_ref=src,
            dst_ref=dst,
            send_sem=send_sem.at[d],
            recv_sem=recv_sem.at[OPPOSITE[d]],
            device_id=target[d],
            device_id_type=pl.DeviceIdType.MESH,
        )

    small[0].wait()
    small[1].wait()
    edge1_v[...] = dot(pack_v[...], x_v[...]).astype(bf16)
    pl.semaphore_wait(barrier, len(target))
    first = [
        remote(x_hbm.at[pl.ds(0, RIM)], rim1_r.at[pl.ds(RIM, RIM)], 0, send1_sem, recv1_sem),
        remote(x_hbm.at[pl.ds(CELLS - RIM, RIM)], rim1_r.at[pl.ds(0, RIM)], 1, send1_sem, recv1_sem),
    ]
    for i, (_, at, size) in enumerate(PIECES):
        other = PIECES[OPPOSITE[2 + i] - 2][1]
        first.append(
            remote(
                edge1_v.at[pl.ds(at, size)], edge1_r.at[pl.ds(other, size)], 2 + i,
                send1_sem, recv1_sem,
            )
        )
    for copy in first:
        copy.start()

    small[2].wait()
    codes = corner_v[...].astype(f32).astype(bf16)
    key_at = lax.broadcasted_iota(jnp.int32, (SPAN, QUAD), 0)
    query_at = lax.broadcasted_iota(jnp.int32, (SPAN, QUAD), 1)
    ext_row, position = key_at >> 4, key_at & 15
    query_row, query_col = (query_at >> 3) & 7, query_at & 7
    key_col = jnp.where(position >= 13, position - 16, position)
    near_row = ext_row - RADIUS - query_row
    near_col = key_col - query_col
    key_row = lev * ROWS + ext_row - RADIUS
    fine = (
        (jnp.abs(near_row) <= RADIUS)
        & (jnp.abs(near_col) <= RADIUS)
        & ((position < 11) | (position > 12))
        & (key_row >= 0)
        & (key_row < levs * ROWS)
    )
    leaves = jnp.where(
        (near_row == 0) | (near_col == 0),
        -1,
        1 + jnp.where(near_row > 0, 2, 0) + jnp.where(near_col > 0, 1, 0),
    ).astype(f32)
    leaves = jnp.where(fine, leaves, -2.0)
    pick_col = lax.broadcasted_iota(jnp.int32, (COLS, QUAD), 0)
    pick_lane = lax.broadcasted_iota(jnp.int32, (COLS, QUAD), 1)
    row_of = lax.broadcasted_iota(jnp.int32, (ROWS, QUAD), 0)
    lane_row = (lax.broadcasted_iota(jnp.int32, (ROWS, QUAD), 1) >> 3) & 7
    for t in range(TILES):
        pick = jnp.where(pick_col == t * TILE + (pick_lane & 7), 1.0, 0.0).astype(bf16)
        spread_codes = dot(codes, pick)
        code = jnp.sum(
            jnp.where(row_of == lane_row, spread_codes, 0.0), axis=0, keepdims=True
        )
        mask_v[t] = jnp.where((leaves == code) | (leaves < -1.5), NEG, 0.0)

    small[3].wait()
    gain = gain_v[...]

    def normed(x):
        inv = lax.rsqrt(jnp.mean(x * x, axis=-1, keepdims=True) + EPSILON)
        return inv, (x * inv * gain).astype(bf16)

    inv_own, own = normed(x_v[...].astype(f32))
    xn_v[...] = own
    inv_v[...] = jnp.broadcast_to(inv_own, (CELLS, 128))

    def by_tiles(y):
        y = y.reshape(ROWS, TILES, TILE, QUAD)
        return jnp.concatenate([y[:, t] for t in range(TILES)], axis=0).reshape(CELLS, QUAD)

    @pl.loop(0, QUADS)
    def _(c):
        weight(c).wait()
        y = dot(xn_v[...], w_v[:, lanes(c)]) * (HEAD_DIM**-0.5)
        q_v[:, lanes(c)] = by_tiles(y).astype(bf16)

    @pl.loop(0, 2 * QUADS)
    def _(c):
        weight(QUADS + c).wait()
        y = dot(xn_v[...], w_v[:, lanes(QUADS + c)])
        kvx_v[pl.ds(RADIUS, ROWS), pl.ds(0, COLS), lanes(c)] = y.reshape(ROWS, COLS, QUAD)

    small[4].wait()
    out_weight.wait()

    @pl.loop(0, QUADS)
    def _(c):
        y = dot(do_v[...], wo_v[lanes(c), :], ROWS_BY_ROWS)
        da_v[:, lanes(c)] = by_tiles(y).astype(bf16)

    small[5].wait()
    small[6].wait()
    for copy in first:
        copy.wait_recv()
    xh_v[pl.ds(0, 2 * RIM)] = normed(rim1_r[...].astype(f32))[1]
    xh_v[pl.ds(2 * RIM, EDGE)] = normed(dot(spread_v[...], edge1_r[...]))[1]

    low_side = lax.broadcasted_iota(jnp.int32, (EXT, TILE, QUAD), 1) < 4

    @pl.loop(0, 2 * QUADS)
    def _(c):
        y = dot(xh_v[...], w_v[:, lanes(QUADS + c)])
        kvx_v[pl.ds(0, RADIUS), pl.ds(0, COLS), lanes(c)] = y[:RIM].reshape(RADIUS, COLS, QUAD)
        kvx_v[pl.ds(RADIUS + ROWS, RADIUS), pl.ds(0, COLS), lanes(c)] = y[RIM : 2 * RIM].reshape(
            RADIUS, COLS, QUAD
        )
        edge = y[2 * RIM :].reshape(EXT, TILE, QUAD)
        for t in range(TILES):
            main = kvx_v[:, pl.ds(t * TILE, TILE), lanes(c)]
            east = edge if t == TILES - 1 else kvx_v[:, pl.ds((t + 1) * TILE, TILE), lanes(c)]
            west = edge if t == 0 else kvx_v[:, pl.ds((t - 1) * TILE, TILE), lanes(c)]
            side = jnp.where(low_side, east, west)
            kt_v[t, :, lanes(c)] = (
                jnp.concatenate([main, side], axis=1).reshape(SPAN, QUAD).astype(bf16)
            )

    lane_head = lax.broadcasted_iota(jnp.int32, (TILE * ROWS, QUAD), 1) >> 6
    head_masks = [jnp.where(lane_head == h, 1.0, 0.0).astype(bf16) for h in range(4)]

    def stacked(y):
        return jnp.concatenate([y * mask for mask in head_masks], axis=0)

    def unstacked(y):
        n = TILE * ROWS
        out = y[:n]
        for h in range(1, 4):
            out = jnp.where(lane_head == h, y[h * n : (h + 1) * n], out)
        return out

    @pl.loop(0, QUADS)
    def _(j):
        atts, gqs = [], []
        for t in range(TILES):
            key, value = kt_v[t, :, lanes(j)], kt_v[t, :, lanes(QUADS + j)]
            cells = pl.ds(t * TILE * ROWS, TILE * ROWS)
            query, d_attn = stacked(q_v[cells, lanes(j)]), stacked(da_v[cells, lanes(j)])
            terms = jnp.exp(dot(key, query, ROWS_BY_ROWS) + mask_v[t])
            weights = terms * (1.0 / jnp.sum(terms, axis=0, keepdims=True))
            weights_b = weights.astype(bf16)
            grad_prob = dot(value, d_attn, ROWS_BY_ROWS)
            delta = jnp.sum(weights * grad_prob, axis=0, keepdims=True)
            dscore = (weights * (grad_prob - delta)).astype(bf16)
            atts.append(unstacked(dot(weights_b, value, COLS_BY_COLS)))
            gqs.append(unstacked(dot(dscore, key, COLS_BY_COLS)) * (HEAD_DIM**-0.5))
            dk_v[t] = dot(dscore, query).reshape(EXT, 2 * TILE, QUAD)
            dv_v[t] = dot(weights_b, d_attn).reshape(EXT, 2 * TILE, QUAD)

        def in_rows(parts):
            parts = [p.reshape(ROWS, TILE, QUAD) for p in parts]
            return jnp.concatenate(parts, axis=1).reshape(CELLS, QUAD).astype(bf16)

        att_v[:, lanes(j)] = in_rows(atts)
        g_v[:, lanes(j)] = in_rows(gqs)
        for d_ref, block in ((dk_v, j), (dv_v, QUADS + j)):
            sides = [d_ref[t, :, pl.ds(TILE, TILE), :] for t in range(TILES)]
            groups = []
            for t in range(TILES):
                low = sides[t - 1] if t > 0 else 0.0
                high = sides[t + 1] if t < TILES - 1 else 0.0
                groups.append(d_ref[t, :, pl.ds(0, TILE), :] + jnp.where(low_side, low, high))
            whole = jnp.concatenate(groups, axis=1)
            g_v[:, lanes(QUADS + block)] = (
                whole[RADIUS : RADIUS + ROWS].reshape(CELLS, QUAD).astype(bf16)
            )
            gh_v[pl.ds(0, RIM), lanes(block)] = whole[:RADIUS].reshape(RIM, QUAD).astype(bf16)
            gh_v[pl.ds(RIM, RIM), lanes(block)] = (
                whole[RADIUS + ROWS :].reshape(RIM, QUAD).astype(bf16)
            )
            edge = jnp.where(low_side, sides[-1], sides[0]).reshape(EDGE, QUAD).astype(bf16)
            gh_v[pl.ds(2 * RIM, PACK), lanes(block)] = dot(spreadt_v[...], edge).astype(bf16)

    @pl.loop(0, QUADS)
    def _(n):
        y = dot(gh_v[...], w_v[lanes(n), pl.ds(WIDTH, 2 * WIDTH)], ROWS_BY_ROWS)
        send2_v[:, lanes(n)] = y.astype(bf16)

    second = [
        remote(send2_v.at[pl.ds(0, RIM)], recv2_v.at[pl.ds(RIM, RIM)], 0, send2_sem, recv2_sem),
        remote(send2_v.at[pl.ds(RIM, RIM)], recv2_v.at[pl.ds(0, RIM)], 1, send2_sem, recv2_sem),
    ]
    for i, (_, at, size) in enumerate(PIECES):
        other = PIECES[OPPOSITE[2 + i] - 2][1]
        second.append(
            remote(
                send2_v.at[pl.ds(2 * RIM + at, size)], recv2_v.at[pl.ds(2 * RIM + other, size)],
                2 + i, send2_sem, recv2_sem,
            )
        )
    for copy in second:
        copy.start()

    @pl.loop(0, QUADS)
    def _(n):
        mixed_v[:, lanes(n)] = dot(att_v[...], wo_v[:, lanes(n)]).astype(bf16)

    mixed_copy = pltpu.make_async_copy(mixed_v, mixed_hbm, out_sem.at[0])
    mixed_copy.start()

    @pl.loop(0, QUADS)
    def _(n):
        dn_v[:, lanes(n)] = dot(g_v[...], w_v[lanes(n), :], ROWS_BY_ROWS)

    small[7].wait()
    for copy in second:
        copy.wait_recv()
    dn_v[pl.ds(0, RIM)] += recv2_v[pl.ds(0, RIM)].astype(f32)
    dn_v[pl.ds(CELLS - RIM, RIM)] += recv2_v[pl.ds(RIM, RIM)].astype(f32)
    scaled = (dn_v[...] + dot(packt_v[...], recv2_v[pl.ds(2 * RIM, PACK)])) * gain
    x = x_v[...].astype(f32)
    inv = inv_v[:, :1]
    mean = jnp.mean(x * scaled, axis=-1, keepdims=True)
    gin_v[...] = (inv * scaled - x * (inv * inv * inv * mean)).astype(bf16)
    gin_copy = pltpu.make_async_copy(gin_v, gin_hbm, out_sem.at[1])
    gin_copy.start()
    mixed_copy.wait()
    gin_copy.wait()
    for copy in first + second:
        copy.wait_send()


def shards(inputs, norm_gain, w_qkv, w_out, d_out, corner):
    assert inputs.shape == (ROWS, COLS, WIDTH), inputs.shape
    f32, bf16 = jnp.float32, jnp.bfloat16
    pack, spread = selections()
    vmem, dma = pltpu.VMEM, pltpu.SemaphoreType.DMA
    anywhere = pl.BlockSpec(memory_space=pl.ANY)
    mixed_out, grad_input = pl.pallas_call(
        kernel,
        out_shape=[jax.ShapeDtypeStruct((CELLS, WIDTH), bf16)] * 2,
        in_specs=[anywhere] * 10,
        out_specs=[anywhere] * 2,
        scratch_shapes=[
            vmem((CELLS, WIDTH), bf16),
            vmem((CELLS, WIDTH), bf16),
            vmem((1, WIDTH), f32),
            vmem((ROWS, COLS), jnp.int32),
            vmem((WIDTH, 3 * WIDTH), bf16),
            vmem((WIDTH, WIDTH), bf16),
            vmem((PACK, CELLS), bf16),
            vmem((CELLS, PACK), bf16),
            vmem((EDGE, PACK), bf16),
            vmem((PACK, EDGE), bf16),
            vmem((CELLS, WIDTH), bf16),
            vmem((2 * RIM + EDGE, WIDTH), bf16),
            vmem((CELLS, 128), f32),
            vmem((CELLS, WIDTH), bf16),
            vmem((CELLS, WIDTH), bf16),
            vmem((EXT, COLS, 2 * WIDTH), f32),
            vmem((TILES, SPAN, 2 * WIDTH), bf16),
            vmem((TILES, SPAN, QUAD), f32),
            vmem((TILES, EXT, 2 * TILE, QUAD), f32),
            vmem((TILES, EXT, 2 * TILE, QUAD), f32),
            vmem((CELLS, WIDTH), bf16),
            vmem((CELLS, 3 * WIDTH), bf16),
            vmem((HALO, 2 * WIDTH), bf16),
            vmem((CELLS, WIDTH), f32),
            vmem((CELLS, WIDTH), bf16),
            vmem((CELLS, WIDTH), bf16),
            vmem((PACK, WIDTH), bf16),
            vmem((2 * RIM, WIDTH), bf16),
            vmem((PACK, WIDTH), bf16),
            vmem((HALO, WIDTH), bf16),
            vmem((HALO, WIDTH), bf16),
            dma((8,)),
            dma((3 * QUADS + 1,)),
            dma((2,)),
            dma((8,)),
            dma((8,)),
            dma((8,)),
            dma((8,)),
        ],
        compiler_params=pltpu.CompilerParams(
            collective_id=0, has_side_effects=True, vmem_limit_bytes=56 * 1024 * 1024
        ),
    )(
        inputs.reshape(CELLS, WIDTH),
        d_out.reshape(CELLS, WIDTH),
        norm_gain.reshape(1, WIDTH),
        corner,
        w_qkv,
        w_out,
        jnp.asarray(pack, bf16),
        jnp.asarray(pack.T, bf16),
        jnp.asarray(spread, bf16),
        jnp.asarray(spread.T, bf16),
    )
    return mixed_out.reshape(inputs.shape), grad_input.reshape(inputs.shape)


def solution(mesh):
    placed = (P("lev", "lon", None), P(), P(), P(), P("lev", "lon", None), P("lev", "lon"))
    return jax.shard_map(
        shards,
        mesh=mesh,
        in_specs=placed,
        out_specs=(P("lev", "lon", None), P("lev", "lon", None)),
        check_vma=False,
    )
```

time: 317 us -> 48.3 us (0.15); the launches traced: 313 us -> 48.1 us
  local copies, waits for them, and re-layouts: 151 us -> 3.74 us
  matrix products: 73.5 us -> 0 us
  other arithmetic: 48.1 us -> 0 us
  Pallas kernels: 0 us -> 43.7 us
  waiting for transfers between devices: 20 us -> 0 us
  starting transfers between devices: 19.5 us -> 0 us
    dot_general x29 -> x0, matrix products: 73.5 us -> none  [the longest x4 15.3 us: forward_band(): jnp.einsum('hqk,qhd->khd', weights_b, g_band, preferred_element_type=jnp....]
    reshape x21 -> x0, local copies, waits for them, and re-layouts: 52.9 us -> none  [the longest x4 12 us: forward_band(): grad_value.reshape(span_rows, ext_cols, width)]
    pallas_call x0 -> x1, Pallas kernels: none -> 43.7 us  [shards(): pl.pallas_call(kernel, out_shape=[jax.ShapeDtypeStruct((CELLS, WIDTH), bf...]
    dynamic_slice x24 -> x0, local copies, waits for them, and re-layouts: 29.2 us -> none  [the longest x4 10.4 us: forward_band(): lax.dynamic_slice_in_dim(key_ext, start, span_rows, 0)]
    transpose x8 -> x0, local copies, waits for them, and re-layouts: 24.6 us -> none  [the longest x4 12.3 us: forward_band(): jnp.einsum('hqk,qhd->khd', weights_b, g_band, preferred_element_type=jnp....]
    ppermute x8 -> x0, waiting for transfers between devices: 20 us -> none  [the longest x2 9.96 us: from_behind(): lax.ppermute(array, axis, [(i, (i + by) % devices) for i in range(devices)])]
    ppermute x8 -> x0, starting transfers between devices: 19.5 us -> none  [the longest x2 9.27 us: padded(): after = lax.ppermute(leading, axis, down)]
    dynamic_update_slice x4 -> x0, other arithmetic: 16.3 us -> none  [forward_band(): lax.dynamic_update_slice(grad_ext, current + addition, (start, 0, 0))]
  transfers between devices with their start and end apart: 8 -> 0, of which waited for: 4 -> 0; matrix products, arithmetic and copies ran while one was open for 5% -> 0% of each run, Pallas kernels for 0% -> 0%
where the time goes in v1:
time: 48.3 us; the launch traced here: 48.1 us
  Pallas kernels  43.7 us (90%)
  local copies, waits for them, and re-layouts  3.74 us (8%)
  between operations  0.64 us (1%)
    pallas_call x1, Pallas kernels, shards(): pl.pallas_call(kernel, out_shape=[jax.ShapeDtypeStruct((CELLS, WIDTH), bf...  43.7 us
    unnamed x2, local copies, waits for them, and re-layouts  3.74 us

profile of v1, /device:TPU:2, one launch (start us, length us, event | category | flops | bytes accessed | tf_op | source)
XLA Modules:
  0.0 48.1 jit_solution(13497491435515161337)
XLA Ops:
  0.6 43.7 %shard_map.113 = (bf16[256,1024]{1,0:T(8,128)(2,1)}, bf16[256,1024]{1,0:T(8,128)(2,1)}) custom-call(bf16[256,1024]{1,0:T(8,128)(2,1)} %bitcast.5, bf16[256,1024]{1,0:T(8,128)(2,1)} %bitcast.6, f32[1,1024]{1,0:T(1,128)} %bitcast.9, s32[8,32]{1,0:T(8,128)} %corner_hbm.1, bf16[1024,3072]{1,0:T(8,128)(2,1)} %wqkv_hbm.1, bf16[1024,1024]{1,0:T(8,128)(2,1)} %wout_hbm.1, ...), custom_call_target="tpu_custom_call" | custom-call | tf_op jit(solution)/shard_map/pallas_call | solution.py:347
  44.4 1.9 %copy.14 = bf16[8,32,1024]{2,1,0:T(8,128)(2,1)} copy(bf16[8,32,1024]{2,1,0:T(8,128)(2,1)} %bitcast.8) | data formatting | bytes 1048576
  46.2 1.9 %copy.15 = bf16[8,32,1024]{2,1,0:T(8,128)(2,1)} copy(bf16[8,32,1024]{2,1,0:T(8,128)(2,1)} %bitcast.7) | data formatting | bytes 1048576

commit v2 on v1

v2 whole, which is shorter than its diff:
```python
import jax
import jax.numpy as jnp
from jax import lax
from jax.experimental import pallas as pl
from jax.experimental.pallas import tpu as pltpu
from jax.sharding import PartitionSpec as P

HEADS = 16
RADIUS = 3
EPSILON = 1e-06

ROWS, COLS, WIDTH = 8, 32, 1024
CELLS = ROWS * COLS
HEAD_DIM = WIDTH // HEADS
QUAD = 4 * HEAD_DIM
QUADS = WIDTH // QUAD
TILE = 8
TILES = COLS // TILE
EXT = ROWS + 2 * RADIUS
SPAN = EXT * 2 * TILE
HALF = COLS // 2
RIM = RADIUS * HALF
SIDE = 64
EDGE = EXT * TILE
PACK = 128
PART = 2 * RIM + EDGE
LATE = 2 * RIM + PACK
NEG = -1e30

PIECES = (
    ((0, -1), 0, 32),
    ((-1, -1), 32, 16),
    ((1, -1), 48, 16),
    ((0, 1), 64, 32),
    ((-1, 1), 96, 16),
    ((1, 1), 112, 16),
)
AROUND = ((-1, 0), (1, 0)) + tuple(p[0] for p in PIECES)
OPPOSITE = tuple(AROUND.index((-d[0], -d[1])) for d in AROUND)


def piece_places(p):
    east, r = p >> 6, p & 63
    north, south = (r >= 32) & (r < 48), r >= 48
    i = jnp.where(south, r - 48, jnp.where(north, r - 32, r))
    row = (i * 43) >> 7
    c = i - 3 * row
    valid = row < jnp.where(north | south, RADIUS, ROWS)
    own_row = row + jnp.where(south, ROWS - RADIUS, 0)
    ext_row = row + jnp.where(south, RADIUS + ROWS, jnp.where(north, 0, RADIUS))
    cell = own_row * COLS + c + (COLS - RADIUS) * east
    edge = ext_row * TILE + c + (TILE - RADIUS) * (1 - east)
    return jnp.where(valid, cell, -1), jnp.where(valid, edge, -1)


def selection(shape, axis, which, first=0):
    p = lax.broadcasted_iota(jnp.int32, shape, axis) + first
    other = lax.broadcasted_iota(jnp.int32, shape, 1 - axis)
    return jnp.where(piece_places(p)[which] == other, 1.0, 0.0).astype(jnp.bfloat16)


def dot(a, b, dims=((1,), (0,))):
    return lax.dot_general(a, b, (dims, ((), ())), preferred_element_type=jnp.float32)


ROWS_BY_ROWS = ((1,), (1,))
COLS_BY_COLS = ((0,), (0,))


def lanes(index, size=QUAD):
    if isinstance(index, int):
        return pl.ds(index * size, size)
    return pl.ds(pl.multiple_of(index * size, size), size)


def kernel(
    x_hbm, do_hbm, gain_hbm, corner_hbm, wqkv_hbm, wout_hbm,
    mixed_o, scaled_o, inv_o,
    x_v, do_v, gain_v, corner_v, w_v, wo_v, pack_v, packt_v, west_v, east_v, spreadt_v,
    xn_v, xh_v, q_v, da_v, kvx_v, kt_v, mask_v, dk_v, dv_v,
    attf_v, gqf_v, att_v, g_v, gh1_v, gh2_v,
    edge1_v, rim1_r, edge1_r, send2a_v, recv2a_r, send2b_v, recv2b_r,
    in_sem, w_sem, send1_sem, recv1_sem, send2_sem, recv2_sem,
):
    f32, bf16 = jnp.float32, jnp.bfloat16
    lon, lev = lax.axis_index("lon"), lax.axis_index("lev")
    lons, levs = lax.axis_size("lon"), lax.axis_size("lev")
    target = [
        {"lon": lax.rem(lon + dx + lons, lons), "lev": lax.rem(lev + dy + levs, levs)}
        for dy, dx in AROUND
    ]
    barrier = pltpu.get_barrier_semaphore()
    for device in target:
        pl.semaphore_signal(
            barrier, inc=1, device_id=device, device_id_type=pl.DeviceIdType.MESH
        )

    small = [
        pltpu.make_async_copy(src, dst, in_sem.at[i])
        for i, (src, dst) in enumerate(
            [
                (x_hbm, x_v), (corner_hbm, corner_v), (gain_hbm, gain_v), (do_hbm, do_v),
            ]
        )
    ]
    for copy in small[:3]:
        copy.start()
    pack_v[...] = selection((PACK, CELLS), 0, 0)

    def weight(c):
        return pltpu.make_async_copy(wqkv_hbm.at[:, lanes(c)], w_v.at[:, lanes(c)], w_sem.at[c])

    out_weight = pltpu.make_async_copy(wout_hbm, wo_v, w_sem.at[3 * QUADS])

    def remote(src, dst, d, slot, send_sem, recv_sem):
        return pltpu.make_async_remote_copy(
            src_ref=src,
            dst_ref=dst,
            send_sem=send_sem.at[slot],
            recv_sem=recv_sem.at[slot],
            device_id=target[d],
            device_id_type=pl.DeviceIdType.MESH,
        )

    def rims(src, dst, slot, send_sem, recv_sem):
        return [
            remote(src[0], dst[1], 0, slot, send_sem, recv_sem),
            remote(src[1], dst[0], 1, slot + 1, send_sem, recv_sem),
        ]

    def pieces(src, dst, base, indices, slot, send_sem, recv_sem):
        copies = []
        for n, i in enumerate(indices):
            at, size = PIECES[i][1:]
            other = PIECES[OPPOSITE[2 + i] - 2][1]
            copies.append(
                remote(
                    src.at[pl.ds(base + at, size)], dst.at[pl.ds(base + other, size)], 2 + i,
                    slot + n, send_sem, recv_sem,
                )
            )
        return copies

    def halves(ref, half):
        columns = pl.ds(half * HALF, HALF)
        return [ref.at[pl.ds(0, RADIUS), columns], ref.at[pl.ds(ROWS - RADIUS, RADIUS), columns]]

    def arrivals(half):
        columns = pl.ds(half * HALF, HALF)
        return [rim1_r.at[pl.ds(0, RADIUS), columns], rim1_r.at[pl.ds(RADIUS, RADIUS), columns]]

    first = [
        rims(halves(x_hbm, p), arrivals(p), 5 * p, send1_sem, recv1_sem)
        + pieces(
            edge1_v, edge1_r, 0, (3, 4, 5) if p == 0 else (0, 1, 2), 5 * p + 2, send1_sem,
            recv1_sem,
        )
        for p in range(2)
    ]
    pl.semaphore_wait(barrier, len(target))
    for copy in first[0][:2]:
        copy.start()
    small[0].wait()
    x_own = x_v[...].reshape(CELLS, WIDTH)
    edge1_v[...] = dot(pack_v[...], x_own).astype(bf16)
    for copy in first[0][2:]:
        copy.start()
    for c in range(3 * QUADS):
        weight(c).start()
    small[3].start()
    out_weight.start()
    packt_v[...] = selection((CELLS, PACK), 1, 0)
    west_v[...] = selection((EDGE, SIDE), 1, 1)
    east_v[...] = selection((EDGE, SIDE), 1, 1, SIDE)
    spreadt_v[...] = selection((PACK, EDGE), 0, 1)

    small[1].wait()
    codes = corner_v[...].astype(f32).astype(bf16)
    key_at = lax.broadcasted_iota(jnp.int32, (SPAN, 128), 0)
    query_at = lax.broadcasted_iota(jnp.int32, (SPAN, 128), 1)
    ext_row, position = key_at >> 4, key_at & 15
    query_row, query_col = (query_at >> 3) & 7, query_at & 7
    key_col = jnp.where(position >= 13, position - 16, position)
    near_row = ext_row - RADIUS - query_row
    near_col = key_col - query_col
    key_row = lev * ROWS + ext_row - RADIUS
    fine = (
        (jnp.abs(near_row) <= RADIUS)
        & (jnp.abs(near_col) <= RADIUS)
        & ((position < 11) | (position > 12))
        & (key_row >= 0)
        & (key_row < levs * ROWS)
    )
    leaves = jnp.where(
        (near_row == 0) | (near_col == 0),
        -1,
        1 + jnp.where(near_row > 0, 2, 0) + jnp.where(near_col > 0, 1, 0),
    ).astype(f32)
    leaves = jnp.where(fine, leaves, -2.0)
    pick_col = lax.broadcasted_iota(jnp.int32, (COLS, 128), 0)
    pick_lane = lax.broadcasted_iota(jnp.int32, (COLS, 128), 1)
    row_of = lax.broadcasted_iota(jnp.int32, (ROWS, 128), 0)
    lane_row = (lax.broadcasted_iota(jnp.int32, (ROWS, 128), 1) >> 3) & 7
    for t in range(TILES):
        pick = jnp.where(pick_col == t * TILE + (pick_lane & 7), 1.0, 0.0).astype(bf16)
        spread_codes = dot(codes, pick)
        code = jnp.sum(
            jnp.where(row_of == lane_row, spread_codes, 0.0), axis=0, keepdims=True
        )
        mask_v[t] = jnp.where((leaves == code) | (leaves < -1.5), NEG, 0.0)

    small[2].wait()
    gain = gain_v[...]

    def normed(x):
        inv = lax.rsqrt(jnp.mean(x * x, axis=-1, keepdims=True) + EPSILON)
        return inv, (x * inv * gain).astype(bf16)

    inv_own, own = normed(x_own.astype(f32))
    xn_v[...] = own
    inv_o[...] = jnp.broadcast_to(inv_own, (CELLS, 128))

    def by_tiles(y):
        y = y.reshape(ROWS, TILES, TILE, QUAD)
        return jnp.concatenate([y[:, t] for t in range(TILES)], axis=0).reshape(CELLS, QUAD)

    @pl.loop(0, QUADS)
    def _(c):
        weight(c).wait()
        y = dot(xn_v[...], w_v[:, lanes(c)]) * (HEAD_DIM**-0.5)
        q_v[:, lanes(c)] = by_tiles(y).astype(bf16)

    for copy in first[1]:
        copy.start()

    @pl.loop(0, 2 * QUADS)
    def _(c):
        weight(QUADS + c).wait()
        y = dot(xn_v[...], w_v[:, lanes(QUADS + c)])
        kvx_v[pl.ds(RADIUS, ROWS), pl.ds(0, COLS), lanes(c)] = y.reshape(ROWS, COLS, QUAD)

    small[3].wait()
    out_weight.wait()

    @pl.loop(0, QUADS)
    def _(c):
        y = dot(do_v[...], wo_v[lanes(c), :], ROWS_BY_ROWS)
        da_v[:, lanes(c)] = by_tiles(y).astype(bf16)

    low_side = lax.broadcasted_iota(jnp.int32, (EXT, TILE, QUAD), 1) < 4

    def received(p, tiles):
        for copy in first[p]:
            copy.wait_recv()
        rim = rim1_r[:, pl.ds(p * HALF, HALF)].reshape(2 * RIM, WIDTH)
        xh_v[pl.ds(0, 2 * RIM)] = normed(rim.astype(f32))[1]
        edge = dot((east_v if p else west_v)[...], edge1_r[pl.ds(p * SIDE, SIDE)])
        xh_v[pl.ds(2 * RIM, EDGE)] = normed(edge)[1]

        @pl.loop(0, 2 * QUADS, unroll=4)
        def _(c):
            y = dot(xh_v[...], w_v[:, lanes(QUADS + c)])
            rim = y[: 2 * RIM].reshape(2, RADIUS, HALF, QUAD)
            kvx_v[pl.ds(0, RADIUS), pl.ds(p * HALF, HALF), lanes(c)] = rim[0]
            kvx_v[pl.ds(RADIUS + ROWS, RADIUS), pl.ds(p * HALF, HALF), lanes(c)] = rim[1]
            kvx_v[:, pl.ds(COLS + p * TILE, TILE), lanes(c)] = y[2 * RIM :].reshape(
                EXT, TILE, QUAD
            )
            for t in tiles:
                main = kvx_v[:, pl.ds(t * TILE, TILE), lanes(c)]
                east = kvx_v[:, pl.ds((t + 1 if t < TILES - 1 else TILES + 1) * TILE, TILE), lanes(c)]
                west = kvx_v[:, pl.ds((t - 1 if t > 0 else TILES) * TILE, TILE), lanes(c)]
                side = jnp.where(low_side, east, west)
                kt_v[t, :, lanes(c)] = (
                    jnp.concatenate([main, side], axis=1).reshape(SPAN, QUAD).astype(bf16)
                )

    lane_head = lax.broadcasted_iota(jnp.int32, (TILE * ROWS, QUAD), 1) >> 6
    head_masks = [jnp.where(lane_head == h, 1.0, 0.0).astype(bf16) for h in range(4)]

    def stacked(y):
        return jnp.concatenate([y * mask for mask in head_masks], axis=0)

    def unstacked(y):
        n = TILE * ROWS
        out = y[:n]
        for h in range(1, 4):
            out = jnp.where(lane_head == h, y[h * n : (h + 1) * n], out)
        return out.reshape(ROWS, TILE, QUAD)

    def attend(t, j):
        key, value = kt_v[t, :, lanes(j)], kt_v[t, :, lanes(QUADS + j)]
        cells, columns = pl.ds(t * TILE * ROWS, TILE * ROWS), pl.ds(t * TILE, TILE)
        query, d_attn = stacked(q_v[cells, lanes(j)]), stacked(da_v[cells, lanes(j)])
        scores = dot(key, query, ROWS_BY_ROWS)
        grad_probs = dot(value, d_attn, ROWS_BY_ROWS)
        mask = mask_v[t]
        weights_b, dscore = [], []
        for half in range(2):
            part = slice(half * 128, (half + 1) * 128)
            terms = jnp.exp(scores[:, part] + mask)
            weights = terms * (1.0 / jnp.sum(terms, axis=0, keepdims=True))
            weights_b.append(weights.astype(bf16))
            grad_prob = grad_probs[:, part]
            delta = jnp.sum(weights * grad_prob, axis=0, keepdims=True)
            dscore.append((weights * (grad_prob - delta)).astype(bf16))
        weights_b, dscore = (jnp.concatenate(y, axis=1) for y in (weights_b, dscore))
        attf_v[:, columns, lanes(j)] = unstacked(dot(weights_b, value, COLS_BY_COLS))
        gqf_v[:, columns, lanes(j)] = unstacked(dot(dscore, key, COLS_BY_COLS)) * (
            HEAD_DIM**-0.5
        )
        dk_v[t, :, :, lanes(j)] = dot(dscore, query).reshape(EXT, 2 * TILE, QUAD)
        dv_v[t, :, :, lanes(j)] = dot(weights_b, d_attn).reshape(EXT, 2 * TILE, QUAD)

    def gathered(j, half, gh_ref):
        for d_ref, block in ((dk_v, j), (dv_v, QUADS + j)):
            groups = []
            for t in (2 * half, 2 * half + 1):
                low = d_ref[t - 1, :, pl.ds(TILE, TILE), lanes(j)] if t > 0 else 0.0
                high = d_ref[t + 1, :, pl.ds(TILE, TILE), lanes(j)] if t < TILES - 1 else 0.0
                main = d_ref[t, :, pl.ds(0, TILE), lanes(j)]
                groups.append(main + jnp.where(low_side, low, high))
            whole = jnp.concatenate(groups, axis=1).astype(bf16)
            g_v[:, pl.ds(half * HALF, HALF), lanes(QUADS + block)] = whole[
                RADIUS : RADIUS + ROWS
            ]
            gh_ref[pl.ds(0, RIM), lanes(block)] = whole[:RADIUS].reshape(RIM, QUAD)
            gh_ref[pl.ds(RIM, RIM), lanes(block)] = whole[RADIUS + ROWS :].reshape(RIM, QUAD)
            if half == 1:
                east = d_ref[TILES - 1, :, pl.ds(TILE, TILE), lanes(j)]
                west = d_ref[0, :, pl.ds(TILE, TILE), lanes(j)]
                edge = jnp.where(low_side, east, west).reshape(EDGE, QUAD).astype(bf16)
                gh_ref[pl.ds(2 * RIM, PACK), lanes(block)] = dot(spreadt_v[...], edge).astype(bf16)

    def projected(gh_ref, out_ref):
        @pl.loop(0, QUADS, unroll=True)
        def _(n):
            y = dot(gh_ref[...], w_v[lanes(n), pl.ds(WIDTH, 2 * WIDTH)], ROWS_BY_ROWS)
            out_ref[:, lanes(n)] = y.astype(bf16)

    received(0, (0,))

    @pl.loop(0, QUADS // 2)
    def _(j):
        attend(0, 2 * j)
        attend(0, 2 * j + 1)

    received(1, (1, 2, 3))

    @pl.loop(0, QUADS)
    def _(j):
        attend(1, j)
        attend(2, j)
        gathered(j, 0, gh1_v)

    projected(gh1_v, send2a_v)
    n_s = [pl.ds(0, RIM), pl.ds(RIM, RIM)]
    second = rims(
        [send2a_v.at[d] for d in n_s], [recv2a_r.at[d] for d in n_s], 0, send2_sem, recv2_sem
    )
    for copy in second:
        copy.start()

    @pl.loop(0, QUADS // 2)
    def _(j):
        for k in range(2):
            attend(3, 2 * j + k)
            gathered(2 * j + k, 1, gh2_v)

    projected(gh2_v, send2b_v)
    third = rims(
        [send2b_v.at[d] for d in n_s], [recv2b_r.at[d] for d in n_s], 2, send2_sem, recv2_sem
    ) + pieces(send2b_v, recv2b_r, 2 * RIM, range(6), 4, send2_sem, recv2_sem)
    for copy in third:
        copy.start()

    att_v[...] = attf_v[...].astype(bf16).reshape(CELLS, WIDTH)
    g_v[:, :, pl.ds(0, WIDTH)] = gqf_v[...].astype(bf16)

    @pl.loop(0, QUADS)
    def _(n):
        mixed_o[:, lanes(n)] = dot(att_v[...], wo_v[:, lanes(n)]).astype(bf16)

    @pl.loop(0, QUADS)
    def _(n):
        scaled_o[:, lanes(n)] = dot(
            g_v[...].reshape(CELLS, 3 * WIDTH), w_v[lanes(n), :], ROWS_BY_ROWS
        )

    for copy in second + third:
        copy.wait_recv()

    def both(rows):
        west, east = (r[rows].astype(f32).reshape(RADIUS, HALF, WIDTH) for r in (recv2a_r, recv2b_r))
        return jnp.concatenate([west, east], axis=1).reshape(2 * RIM, WIDTH)

    scaled_o[pl.ds(0, 2 * RIM)] += both(n_s[0])
    scaled_o[pl.ds(CELLS - 2 * RIM, 2 * RIM)] += both(n_s[1])
    edges = dot(packt_v[...], recv2b_r[pl.ds(2 * RIM, PACK)])
    scaled_o[...] = (scaled_o[...] + edges) * gain
    for copy in first[0] + first[1] + second + third:
        copy.wait_send()


def finish(x_ref, mixed_ref, scaled_ref, inv_ref, mixed_hbm, gin_hbm, gin_v, sem):
    mixed_copy = pltpu.make_async_copy(mixed_ref, mixed_hbm, sem.at[0])
    mixed_copy.start()
    blocks = 4
    size = CELLS // blocks
    copies = []
    for b in range(blocks):
        rows = pl.ds(b * size, size)
        x, scaled, inv = x_ref[rows].astype(jnp.float32), scaled_ref[rows], inv_ref[rows][:, :1]
        mean = jnp.mean(x * scaled, axis=-1, keepdims=True)
        gin_v[rows] = (inv * scaled - x * (inv * inv * inv * mean)).astype(gin_v.dtype)
        copies.append(pltpu.make_async_copy(gin_v.at[rows], gin_hbm.at[rows], sem.at[1 + b]))
        copies[-1].start()
    for copy in [mixed_copy] + copies:
        copy.wait()


def shards(inputs, norm_gain, w_qkv, w_out, d_out, corner):
    assert inputs.shape == (ROWS, COLS, WIDTH), inputs.shape
    f32, bf16 = jnp.float32, jnp.bfloat16
    vmem, dma = pltpu.VMEM, pltpu.SemaphoreType.DMA
    anywhere = pl.BlockSpec(memory_space=pl.ANY)
    inside = pl.BlockSpec(memory_space=pltpu.VMEM)
    mixed, scaled, inv = pl.pallas_call(
        kernel,
        out_shape=[
            vmem((CELLS, WIDTH), bf16),
            vmem((CELLS, WIDTH), f32),
            vmem((CELLS, 128), f32),
        ],
        in_specs=[anywhere] * 6,
        out_specs=[inside] * 3,
        scratch_shapes=[
            vmem((ROWS, COLS, WIDTH), bf16),
            vmem((CELLS, WIDTH), bf16),
            vmem((1, WIDTH), f32),
            vmem((ROWS, COLS), jnp.int32),
            vmem((WIDTH, 3 * WIDTH), bf16),
            vmem((WIDTH, WIDTH), bf16),
            vmem((PACK, CELLS), bf16),
            vmem((CELLS, PACK), bf16),
            vmem((EDGE, SIDE), bf16),
            vmem((EDGE, SIDE), bf16),
            vmem((PACK, EDGE), bf16),
            vmem((CELLS, WIDTH), bf16),
            vmem((PART, WIDTH), bf16),
            vmem((CELLS, WIDTH), bf16),
            vmem((CELLS, WIDTH), bf16),
            vmem((EXT, COLS + 2 * TILE, 2 * WIDTH), f32),
            vmem((TILES, SPAN, 2 * WIDTH), bf16),
            vmem((TILES, SPAN, 128), f32),
            vmem((TILES, EXT, 2 * TILE, WIDTH), f32),
            vmem((TILES, EXT, 2 * TILE, WIDTH), f32),
            vmem((ROWS, COLS, WIDTH), f32),
            vmem((ROWS, COLS, WIDTH), f32),
            vmem((CELLS, WIDTH), bf16),
            vmem((ROWS, COLS, 3 * WIDTH), bf16),
            vmem((2 * RIM, 2 * WIDTH), bf16),
            vmem((LATE, 2 * WIDTH), bf16),
            vmem((PACK, WIDTH), bf16),
            vmem((2 * RADIUS, COLS, WIDTH), bf16),
            vmem((PACK, WIDTH), bf16),
            vmem((2 * RIM, WIDTH), bf16),
            vmem((2 * RIM, WIDTH), bf16),
            vmem((LATE, WIDTH), bf16),
            vmem((LATE, WIDTH), bf16),
            dma((4,)),
            dma((3 * QUADS + 1,)),
            dma((10,)),
            dma((10,)),
            dma((10,)),
            dma((10,)),
        ],
        compiler_params=pltpu.CompilerParams(
            collective_id=0, has_side_effects=True, vmem_limit_bytes=61 * 1024 * 1024
        ),
    )(
        inputs,
        d_out.reshape(CELLS, WIDTH),
        norm_gain.reshape(1, WIDTH),
        corner,
        w_qkv,
        w_out,
    )
    mixed_out, grad_input = pl.pallas_call(
        finish,
        out_shape=[jax.ShapeDtypeStruct((CELLS, WIDTH), bf16)] * 2,
        in_specs=[inside] * 4,
        out_specs=[anywhere] * 2,
        scratch_shapes=[vmem((CELLS, WIDTH), bf16), dma((5,))],
        compiler_params=pltpu.CompilerParams(vmem_limit_bytes=16 * 1024 * 1024),
    )(inputs.reshape(CELLS, WIDTH), mixed, scaled, inv)
    return mixed_out.reshape(inputs.shape), grad_input.reshape(inputs.shape)


def solution(mesh):
    placed = (P("lev", "lon", None), P(), P(), P(), P("lev", "lon", None), P("lev", "lon"))
    return jax.shard_map(
        shards,
        mesh=mesh,
        in_specs=placed,
        out_specs=(P("lev", "lon", None), P("lev", "lon", None)),
        check_vma=False,
    )
```

time: 48.3 us -> 42.1 us (0.87)
  the two profiles are of different devices: /device:TPU:2 before, /device:TPU:1 now
where the time goes in v2:
time: 42.1 us
  Pallas kernels  41.4 us (98%)
  between operations  0.66 us (2%)
    pallas_call x1, Pallas kernels, shards(): pl.pallas_call(kernel, out_shape=[vmem((CELLS, WIDTH), bf16), vmem((CELLS...  40.3 us
    pallas_call x1, Pallas kernels, shards(): pl.pallas_call(finish, out_shape=[jax.ShapeDtypeStruct((CELLS, WIDTH), bf...  1.07 us

profile of v2, /device:TPU:1, one launch (start us, length us, event | category | flops | bytes accessed | tf_op | source)
XLA Modules:
  0.0 42.1 jit_solution(11036307745958811917)
XLA Ops:
  0.6 0.0 copy-start
  0.6 40.3 %shard_map.77 = (bf16[256,1024]{1,0:T(8,128)(2,1)S(1)}, f32[256,1024]{1,0:T(8,128)S(1)}, f32[256,128]{1,0:T(8,128)S(1)}) custom-call(bf16[8,32,1024]{2,1,0:T(8,128)(2,1)} %x_hbm.1, bf16[256,1024]{1,0:T(8,128)(2,1)} %bitcast.6, f32[1,1024]{1,0:T(1,128)} %bitcast.7, s32[8,32]{1,0:T(8,128)} %corner_hbm.1, bf16[1024,3072]{1,0:T(8,128)(2,1)} %wqkv_hbm.1, ...), custom_call_target="tpu_custom_call" | custom-call | tf_op jit(solution)/shard_map/pallas_call | solution.py:428
  41.0 0.0 copy-done
  41.0 1.1 %shard_map.78 = (bf16[256,1024]{1,0:T(8,128)(2,1)}, bf16[256,1024]{1,0:T(8,128)(2,1)}) custom-call(bf16[256,1024]{1,0:T(8,128)(2,1)S(1)} %bitcast.5, bf16[256,1024]{1,0:T(8,128)(2,1)S(1)} %get-tuple-element.7.mixed_ref, f32[256,1024]{1,0:T(8,128)S(1)} %get-tuple-element.8.scaled_ref, f32[256,128]{1,0:T(8,128)S(1)} %get-tuple-element.9.inv_ref), custom_call_target="tpu_custom_call" | custom-call | tf_op jit(solution)/shard_map/pallas_call | solution.py:489
Async XLA Ops:
  0.6 40.3 %copy-start = (bf16[8,32,1024]{2,1,0:T(8,128)(2,1)S(1)}, bf16[8,32,1024]{2,1,0:T(8,128)(2,1)}, u32[]{:S(2)}) copy-start(bf16[8,32,1024]{2,1,0:T(8,128)(2,1)} %x_hbm.1) | copy-start | bytes 1572868

commit v3 on v2

--- a/solution.py
+++ b/solution.py
@@ -79,6 +79,7 @@
     x_v, do_v, gain_v, corner_v, w_v, wo_v, pack_v, packt_v, west_v, east_v, spreadt_v,
     xn_v, xh_v, q_v, da_v, kvx_v, kt_v, mask_v, dk_v, dv_v,
     attf_v, gqf_v, att_v, g_v, gh1_v, gh2_v,
+    score_v, prob_v, weight_v, dscore_v,
     edge1_v, rim1_r, edge1_r, send2a_v, recv2a_r, send2b_v, recv2b_r,
     in_sem, w_sem, send1_sem, recv1_sem, send2_sem, recv2_sem,
 ):
@@ -224,7 +225,7 @@
         y = y.reshape(ROWS, TILES, TILE, QUAD)
         return jnp.concatenate([y[:, t] for t in range(TILES)], axis=0).reshape(CELLS, QUAD)
 
-    @pl.loop(0, QUADS)
+    @pl.loop(0, QUADS, unroll=True)
     def _(c):
         weight(c).wait()
         y = dot(xn_v[...], w_v[:, lanes(c)]) * (HEAD_DIM**-0.5)
@@ -233,7 +234,7 @@
     for copy in first[1]:
         copy.start()
 
-    @pl.loop(0, 2 * QUADS)
+    @pl.loop(0, 2 * QUADS, unroll=True)
     def _(c):
         weight(QUADS + c).wait()
         y = dot(xn_v[...], w_v[:, lanes(QUADS + c)])
@@ -242,7 +243,7 @@
     small[3].wait()
     out_weight.wait()
 
-    @pl.loop(0, QUADS)
+    @pl.loop(0, QUADS, unroll=True)
     def _(c):
         y = dot(do_v[...], wo_v[lanes(c), :], ROWS_BY_ROWS)
         da_v[:, lanes(c)] = by_tiles(y).astype(bf16)
@@ -257,7 +258,7 @@
         edge = dot((east_v if p else west_v)[...], edge1_r[pl.ds(p * SIDE, SIDE)])
         xh_v[pl.ds(2 * RIM, EDGE)] = normed(edge)[1]
 
-        @pl.loop(0, 2 * QUADS, unroll=4)
+        @pl.loop(0, 2 * QUADS, unroll=True)
         def _(c):
             y = dot(xh_v[...], w_v[:, lanes(QUADS + c)])
             rim = y[: 2 * RIM].reshape(2, RADIUS, HALF, QUAD)
@@ -288,29 +289,58 @@
             out = jnp.where(lane_head == h, y[h * n : (h + 1) * n], out)
         return out.reshape(ROWS, TILE, QUAD)
 
-    def attend(t, j):
+    chunks = [pl.ds(r, 32) for r in range(0, SPAN, 32)]
+
+    def folded(y):
+        return jnp.sum(y.reshape(4, 8, QUAD), axis=0)
+
+    def score(slot, t, j):
+        key, value = kt_v[t, :, lanes(j)], kt_v[t, :, lanes(QUADS + j)]
+        cells = pl.ds(t * TILE * ROWS, TILE * ROWS)
+        query, d_attn = stacked(q_v[cells, lanes(j)]), stacked(da_v[cells, lanes(j)])
+        score_v[slot] = dot(key, query, ROWS_BY_ROWS)
+        prob_v[slot] = dot(value, d_attn, ROWS_BY_ROWS)
+
+    def weigh(slot, t):
+        total = jnp.zeros((8, QUAD), f32)
+        for rows in chunks:
+            mask = mask_v[t, rows]
+            terms = jnp.exp(score_v[slot, rows] + jnp.concatenate([mask, mask], axis=1))
+            score_v[slot, rows] = terms
+            total += folded(terms)
+        scale = 1.0 / jnp.sum(total, axis=0, keepdims=True)
+        total = jnp.zeros((8, QUAD), f32)
+        for rows in chunks:
+            weights = score_v[slot, rows] * scale
+            weight_v[slot, rows] = weights.astype(bf16)
+            total += folded(weights * prob_v[slot, rows])
+        delta = jnp.sum(total, axis=0, keepdims=True)
+        for rows in chunks:
+            weights = score_v[slot, rows] * scale
+            dscore_v[slot, rows] = (weights * (prob_v[slot, rows] - delta)).astype(bf16)
+
+    def apply(slot, t, j):
         key, value = kt_v[t, :, lanes(j)], kt_v[t, :, lanes(QUADS + j)]
         cells, columns = pl.ds(t * TILE * ROWS, TILE * ROWS), pl.ds(t * TILE, TILE)
         query, d_attn = stacked(q_v[cells, lanes(j)]), stacked(da_v[cells, lanes(j)])
-        scores = dot(key, query, ROWS_BY_ROWS)
-        grad_probs = dot(value, d_attn, ROWS_BY_ROWS)
-        mask = mask_v[t]
-        weights_b, dscore = [], []
-        for half in range(2):
-            part = slice(half * 128, (half + 1) * 128)
-            terms = jnp.exp(scores[:, part] + mask)
-            weights = terms * (1.0 / jnp.sum(terms, axis=0, keepdims=True))
-            weights_b.append(weights.astype(bf16))
-            grad_prob = grad_probs[:, part]
-            delta = jnp.sum(weights * grad_prob, axis=0, keepdims=True)
-            dscore.append((weights * (grad_prob - delta)).astype(bf16))
-        weights_b, dscore = (jnp.concatenate(y, axis=1) for y in (weights_b, dscore))
+        weights_b, dscore = weight_v[slot], dscore_v[slot]
         attf_v[:, columns, lanes(j)] = unstacked(dot(weights_b, value, COLS_BY_COLS))
         gqf_v[:, columns, lanes(j)] = unstacked(dot(dscore, key, COLS_BY_COLS)) * (
             HEAD_DIM**-0.5
         )
         dk_v[t, :, :, lanes(j)] = dot(dscore, query).reshape(EXT, 2 * TILE, QUAD)
         dv_v[t, :, :, lanes(j)] = dot(weights_b, d_attn).reshape(EXT, 2 * TILE, QUAD)
+
+    def attend(items, after=None):
+        for i in range(len(items) + 2):
+            if i < len(items):
+                score(i % 2, *items[i])
+            if 0 <= i - 2:
+                apply(i % 2, *items[i - 2])
+                if after:
+                    after(*items[i - 2])
+            if 0 <= i - 1 < len(items):
+                weigh((i - 1) % 2, items[i - 1][0])
 
     def gathered(j, half, gh_ref):
         for d_ref, block in ((dk_v, j), (dv_v, QUADS + j)):
@@ -340,19 +370,13 @@
 
     received(0, (0,))
 
-    @pl.loop(0, QUADS // 2)
-    def _(j):
-        attend(0, 2 * j)
-        attend(0, 2 * j + 1)
-
+    attend([(0, j) for j in range(QUADS)])
     received(1, (1, 2, 3))
 
-    @pl.loop(0, QUADS)
-    def _(j):
-        attend(1, j)
-        attend(2, j)
-        gathered(j, 0, gh1_v)
-
+    attend(
+        [(t, j) for j in range(QUADS) for t in (1, 2)],
+        lambda t, j: gathered(j, 0, gh1_v) if t == 2 else None,
+    )
     projected(gh1_v, send2a_v)
     n_s = [pl.ds(0, RIM), pl.ds(RIM, RIM)]
     second = rims(
@@ -361,12 +385,7 @@
     for copy in second:
         copy.start()
 
-    @pl.loop(0, QUADS // 2)
-    def _(j):
-        for k in range(2):
-            attend(3, 2 * j + k)
-            gathered(2 * j + k, 1, gh2_v)
-
+    attend([(3, j) for j in range(QUADS)], lambda t, j: gathered(j, 1, gh2_v))
     projected(gh2_v, send2b_v)
     third = rims(
         [send2b_v.at[d] for d in n_s], [recv2b_r.at[d] for d in n_s], 2, send2_sem, recv2_sem
@@ -377,11 +396,11 @@
     att_v[...] = attf_v[...].astype(bf16).reshape(CELLS, WIDTH)
     g_v[:, :, pl.ds(0, WIDTH)] = gqf_v[...].astype(bf16)
 
-    @pl.loop(0, QUADS)
+    @pl.loop(0, QUADS, unroll=True)
     def _(n):
         mixed_o[:, lanes(n)] = dot(att_v[...], wo_v[:, lanes(n)]).astype(bf16)
 
-    @pl.loop(0, QUADS)
+    @pl.loop(0, QUADS, unroll=True)
     def _(n):
         scaled_o[:, lanes(n)] = dot(
             g_v[...].reshape(CELLS, 3 * WIDTH), w_v[lanes(n), :], ROWS_BY_ROWS
@@ -461,6 +480,10 @@
             vmem((ROWS, COLS, 3 * WIDTH), bf16),
             vmem((2 * RIM, 2 * WIDTH), bf16),
             vmem((LATE, 2 * WIDTH), bf16),
+            vmem((2, SPAN, QUAD), f32),
+            vmem((2, SPAN, QUAD), f32),
+            vmem((2, SPAN, QUAD), bf16),
+            vmem((2, SPAN, QUAD), bf16),
             vmem((PACK, WIDTH), bf16),
             vmem((2 * RADIUS, COLS, WIDTH), bf16),
             vmem((PACK, WIDTH), bf16),

time: 42.1 us -> 37.1 us (0.88)
  the two profiles are of different devices: /device:TPU:1 before, /device:TPU:2 now
where the time goes in v3:
time: 37.1 us; the launch traced here: 37 us
  Pallas kernels  36.2 us (98%)
  between operations  0.82 us (2%)
    pallas_call x1, Pallas kernels, shards(): pl.pallas_call(kernel, out_shape=[vmem((CELLS, WIDTH), bf16), vmem((CELLS...  35.1 us
    pallas_call x1, Pallas kernels, shards(): pl.pallas_call(finish, out_shape=[jax.ShapeDtypeStruct((CELLS, WIDTH), bf...  1.07 us

profile of v3, /device:TPU:2, one launch (start us, length us, event | category | flops | bytes accessed | tf_op | source)
XLA Modules:
  0.0 37.0 jit_solution(4905063326280988428)
XLA Ops:
  0.6 0.0 copy-start
  0.6 35.1 %shard_map.77 = (bf16[256,1024]{1,0:T(8,128)(2,1)S(1)}, f32[256,1024]{1,0:T(8,128)S(1)}, f32[256,128]{1,0:T(8,128)S(1)}) custom-call(bf16[8,32,1024]{2,1,0:T(8,128)(2,1)} %x_hbm.1, bf16[256,1024]{1,0:T(8,128)(2,1)} %bitcast.6, f32[1,1024]{1,0:T(1,128)} %bitcast.7, s32[8,32]{1,0:T(8,128)} %corner_hbm.1, bf16[1024,3072]{1,0:T(8,128)(2,1)} %wqkv_hbm.1, ...), custom_call_target="tpu_custom_call" | custom-call | tf_op jit(solution)/shard_map/pallas_call | solution.py:447
  35.8 0.0 copy-done
  35.8 1.1 %shard_map.78 = (bf16[256,1024]{1,0:T(8,128)(2,1)}, bf16[256,1024]{1,0:T(8,128)(2,1)}) custom-call(bf16[256,1024]{1,0:T(8,128)(2,1)S(1)} %bitcast.5, bf16[256,1024]{1,0:T(8,128)(2,1)S(1)} %get-tuple-element.7.mixed_ref, f32[256,1024]{1,0:T(8,128)S(1)} %get-tuple-element.8.scaled_ref, f32[256,128]{1,0:T(8,128)S(1)} %get-tuple-element.9.inv_ref), custom_call_target="tpu_custom_call" | custom-call | tf_op jit(solution)/shard_map/pallas_call | solution.py:512
Async XLA Ops:
  0.6 35.2 %copy-start = (bf16[8,32,1024]{2,1,0:T(8,128)(2,1)S(1)}, bf16[8,32,1024]{2,1,0:T(8,128)(2,1)}, u32[]{:S(2)}) copy-start(bf16[8,32,1024]{2,1,0:T(8,128)(2,1)} %x_hbm.1) | copy-start | bytes 1572868

commit v4 on v3

--- a/solution.py
+++ b/solution.py
@@ -225,18 +225,18 @@
         y = y.reshape(ROWS, TILES, TILE, QUAD)
         return jnp.concatenate([y[:, t] for t in range(TILES)], axis=0).reshape(CELLS, QUAD)
 
-    @pl.loop(0, QUADS, unroll=True)
-    def _(c):
+    for c in range(QUADS):
         weight(c).wait()
+    for c in range(QUADS):
         y = dot(xn_v[...], w_v[:, lanes(c)]) * (HEAD_DIM**-0.5)
         q_v[:, lanes(c)] = by_tiles(y).astype(bf16)
 
     for copy in first[1]:
         copy.start()
 
-    @pl.loop(0, 2 * QUADS, unroll=True)
-    def _(c):
-        weight(QUADS + c).wait()
+    for c in range(QUADS, 3 * QUADS):
+        weight(c).wait()
+    for c in range(2 * QUADS):
         y = dot(xn_v[...], w_v[:, lanes(QUADS + c)])
         kvx_v[pl.ds(RADIUS, ROWS), pl.ds(0, COLS), lanes(c)] = y.reshape(ROWS, COLS, QUAD)
 
@@ -301,7 +301,7 @@
         score_v[slot] = dot(key, query, ROWS_BY_ROWS)
         prob_v[slot] = dot(value, d_attn, ROWS_BY_ROWS)
 
-    def weigh(slot, t):
+    def weigh(slot, i, t):
         total = jnp.zeros((8, QUAD), f32)
         for rows in chunks:
             mask = mask_v[t, rows]
@@ -312,35 +312,37 @@
         total = jnp.zeros((8, QUAD), f32)
         for rows in chunks:
             weights = score_v[slot, rows] * scale
-            weight_v[slot, rows] = weights.astype(bf16)
+            weight_v[i, rows] = weights.astype(bf16)
             total += folded(weights * prob_v[slot, rows])
         delta = jnp.sum(total, axis=0, keepdims=True)
         for rows in chunks:
             weights = score_v[slot, rows] * scale
-            dscore_v[slot, rows] = (weights * (prob_v[slot, rows] - delta)).astype(bf16)
-
-    def apply(slot, t, j):
+            dscore_v[i, rows] = (weights * (prob_v[slot, rows] - delta)).astype(bf16)
+
+    def to_keys(i, t, j):
+        cells = pl.ds(t * TILE * ROWS, TILE * ROWS)
+        query, d_attn = stacked(q_v[cells, lanes(j)]), stacked(da_v[cells, lanes(j)])
+        dk_v[t, :, :, lanes(j)] = dot(dscore_v[i], query).reshape(EXT, 2 * TILE, QUAD)
+        dv_v[t, :, :, lanes(j)] = dot(weight_v[i], d_attn).reshape(EXT, 2 * TILE, QUAD)
+
+    def to_queries(i, t, j):
         key, value = kt_v[t, :, lanes(j)], kt_v[t, :, lanes(QUADS + j)]
-        cells, columns = pl.ds(t * TILE * ROWS, TILE * ROWS), pl.ds(t * TILE, TILE)
-        query, d_attn = stacked(q_v[cells, lanes(j)]), stacked(da_v[cells, lanes(j)])
-        weights_b, dscore = weight_v[slot], dscore_v[slot]
-        attf_v[:, columns, lanes(j)] = unstacked(dot(weights_b, value, COLS_BY_COLS))
-        gqf_v[:, columns, lanes(j)] = unstacked(dot(dscore, key, COLS_BY_COLS)) * (
+        columns = pl.ds(t * TILE, TILE)
+        attf_v[:, columns, lanes(j)] = unstacked(dot(weight_v[i].T, value))
+        gqf_v[:, columns, lanes(j)] = unstacked(dot(dscore_v[i].T, key)) * (
             HEAD_DIM**-0.5
         )
-        dk_v[t, :, :, lanes(j)] = dot(dscore, query).reshape(EXT, 2 * TILE, QUAD)
-        dv_v[t, :, :, lanes(j)] = dot(weights_b, d_attn).reshape(EXT, 2 * TILE, QUAD)
-
-    def attend(items, after=None):
+
+    def attend(items, before, after):
         for i in range(len(items) + 2):
             if i < len(items):
+                before(*items[i])
                 score(i % 2, *items[i])
             if 0 <= i - 2:
-                apply(i % 2, *items[i - 2])
-                if after:
-                    after(*items[i - 2])
+                to_keys(i - 2, *items[i - 2])
+                after(*items[i - 2])
             if 0 <= i - 1 < len(items):
-                weigh((i - 1) % 2, items[i - 1][0])
+                weigh((i - 1) % 2, i - 1, items[i - 1][0])
 
     def gathered(j, half, gh_ref):
         for d_ref, block in ((dk_v, j), (dv_v, QUADS + j)):
@@ -368,42 +370,56 @@
             y = dot(gh_ref[...], w_v[lanes(n), pl.ds(WIDTH, 2 * WIDTH)], ROWS_BY_ROWS)
             out_ref[:, lanes(n)] = y.astype(bf16)
 
-    received(0, (0,))
-
-    attend([(0, j) for j in range(QUADS)])
-    received(1, (1, 2, 3))
-
-    attend(
-        [(t, j) for j in range(QUADS) for t in (1, 2)],
-        lambda t, j: gathered(j, 0, gh1_v) if t == 2 else None,
-    )
-    projected(gh1_v, send2a_v)
     n_s = [pl.ds(0, RIM), pl.ds(RIM, RIM)]
     second = rims(
         [send2a_v.at[d] for d in n_s], [recv2a_r.at[d] for d in n_s], 0, send2_sem, recv2_sem
     )
-    for copy in second:
-        copy.start()
-
-    attend([(3, j) for j in range(QUADS)], lambda t, j: gathered(j, 1, gh2_v))
-    projected(gh2_v, send2b_v)
     third = rims(
         [send2b_v.at[d] for d in n_s], [recv2b_r.at[d] for d in n_s], 2, send2_sem, recv2_sem
     ) + pieces(send2b_v, recv2b_r, 2 * RIM, range(6), 4, send2_sem, recv2_sem)
+
+    def before(t, j):
+        if (t, j) == (0, 0):
+            received(0, (0,))
+        if (t, j) == (1, 0):
+            received(1, (1, 2, 3))
+
+    def after(t, j):
+        if t == 2:
+            gathered(j, 0, gh1_v)
+        if t == 3:
+            gathered(j, 1, gh2_v)
+        if (t, j) == (2, QUADS - 1):
+            projected(gh1_v, send2a_v)
+            for copy in second:
+                copy.start()
+
+    items = (
+        [(0, j) for j in range(QUADS)]
+        + [(t, j) for j in range(QUADS) for t in (1, 2)]
+        + [(3, j) for j in range(QUADS)]
+    )
+    attend(items, before, after)
+    projected(gh2_v, send2b_v)
     for copy in third:
         copy.start()
 
+    for n in range(QUADS):
+        for i in range(n * len(items) // QUADS, (n + 1) * len(items) // QUADS):
+            to_queries(i, *items[i])
+        scaled_o[:, lanes(n)] = dot(
+            g_v[:, :, pl.ds(WIDTH, 2 * WIDTH)].reshape(CELLS, 2 * WIDTH),
+            w_v[lanes(n), pl.ds(WIDTH, 2 * WIDTH)],
+            ROWS_BY_ROWS,
+        )
     att_v[...] = attf_v[...].astype(bf16).reshape(CELLS, WIDTH)
     g_v[:, :, pl.ds(0, WIDTH)] = gqf_v[...].astype(bf16)
-
-    @pl.loop(0, QUADS, unroll=True)
-    def _(n):
+    for n in range(QUADS):
         mixed_o[:, lanes(n)] = dot(att_v[...], wo_v[:, lanes(n)]).astype(bf16)
-
-    @pl.loop(0, QUADS, unroll=True)
-    def _(n):
-        scaled_o[:, lanes(n)] = dot(
-            g_v[...].reshape(CELLS, 3 * WIDTH), w_v[lanes(n), :], ROWS_BY_ROWS
+        scaled_o[:, lanes(n)] += dot(
+            g_v[:, :, pl.ds(0, WIDTH)].reshape(CELLS, WIDTH),
+            w_v[lanes(n), pl.ds(0, WIDTH)],
+            ROWS_BY_ROWS,
         )
 
     for copy in second + third:
@@ -482,8 +498,8 @@
             vmem((LATE, 2 * WIDTH), bf16),
             vmem((2, SPAN, QUAD), f32),
             vmem((2, SPAN, QUAD), f32),
-            vmem((2, SPAN, QUAD), bf16),
-            vmem((2, SPAN, QUAD), bf16),
+            vmem((TILES * QUADS, SPAN, QUAD), bf16),
+            vmem((TILES * QUADS, SPAN, QUAD), bf16),
             vmem((PACK, WIDTH), bf16),
             vmem((2 * RADIUS, COLS, WIDTH), bf16),
             vmem((PACK, WIDTH), bf16),

time: 37.1 us -> 36.4 us (0.981)
  Pallas kernels: 36.2 us -> 35.7 us
    pallas_call x1, Pallas kernels: 35.1 us -> 34.6 us  [shards(): pl.pallas_call(kernel, out_shape=[vmem((CELLS, WIDTH), bf16), vmem((CELLS...]
where the time goes in v4:
time: 36.4 us; the launch traced here: 36.3 us
  Pallas kernels  35.7 us (98%)
  between operations  0.66 us (2%)
    pallas_call x1, Pallas kernels, shards(): pl.pallas_call(kernel, out_shape=[vmem((CELLS, WIDTH), bf16), vmem((CELLS...  34.6 us
    pallas_call x1, Pallas kernels, shards(): pl.pallas_call(finish, out_shape=[jax.ShapeDtypeStruct((CELLS, WIDTH), bf...  1.07 us

profile of v4, /device:TPU:2, one launch (start us, length us, event | category | flops | bytes accessed | tf_op | source)
XLA Modules:
  0.0 36.3 jit_solution(17023672796076244704)
XLA Ops:
  0.6 0.0 copy-start
  0.6 34.6 %shard_map.77 = (bf16[256,1024]{1,0:T(8,128)(2,1)S(1)}, f32[256,1024]{1,0:T(8,128)S(1)}, f32[256,128]{1,0:T(8,128)S(1)}) custom-call(bf16[8,32,1024]{2,1,0:T(8,128)(2,1)} %x_hbm.1, bf16[256,1024]{1,0:T(8,128)(2,1)} %bitcast.6, f32[1,1024]{1,0:T(1,128)} %bitcast.7, s32[8,32]{1,0:T(8,128)} %corner_hbm.1, bf16[1024,3072]{1,0:T(8,128)(2,1)} %wqkv_hbm.1, ...), custom_call_target="tpu_custom_call" | custom-call | tf_op jit(solution)/shard_map/pallas_call | solution.py:463
  35.2 0.0 copy-done
  35.3 1.1 %shard_map.78 = (bf16[256,1024]{1,0:T(8,128)(2,1)}, bf16[256,1024]{1,0:T(8,128)(2,1)}) custom-call(bf16[256,1024]{1,0:T(8,128)(2,1)S(1)} %bitcast.5, bf16[256,1024]{1,0:T(8,128)(2,1)S(1)} %get-tuple-element.7.mixed_ref, f32[256,1024]{1,0:T(8,128)S(1)} %get-tuple-element.8.scaled_ref, f32[256,128]{1,0:T(8,128)S(1)} %get-tuple-element.9.inv_ref), custom_call_target="tpu_custom_call" | custom-call | tf_op jit(solution)/shard_map/pallas_call | solution.py:528
Async XLA Ops:
  0.6 34.6 %copy-start = (bf16[8,32,1024]{2,1,0:T(8,128)(2,1)S(1)}, bf16[8,32,1024]{2,1,0:T(8,128)(2,1)}, u32[]{:S(2)}) copy-start(bf16[8,32,1024]{2,1,0:T(8,128)(2,1)} %x_hbm.1) | copy-start | bytes 1572868

commit v5 on v4

--- a/solution.py
+++ b/solution.py
@@ -158,15 +158,15 @@
         )
         for p in range(2)
     ]
-    pl.semaphore_wait(barrier, len(target))
-    for copy in first[0][:2]:
-        copy.start()
+    for c in range(2 * QUADS):
+        weight(c).start()
     small[0].wait()
     x_own = x_v[...].reshape(CELLS, WIDTH)
     edge1_v[...] = dot(pack_v[...], x_own).astype(bf16)
-    for copy in first[0][2:]:
+    pl.semaphore_wait(barrier, len(target))
+    for copy in first[0] + first[1]:
         copy.start()
-    for c in range(3 * QUADS):
+    for c in range(2 * QUADS, 3 * QUADS):
         weight(c).start()
     small[3].start()
     out_weight.start()
@@ -231,9 +231,6 @@
         y = dot(xn_v[...], w_v[:, lanes(c)]) * (HEAD_DIM**-0.5)
         q_v[:, lanes(c)] = by_tiles(y).astype(bf16)
 
-    for copy in first[1]:
-        copy.start()
-
     for c in range(QUADS, 3 * QUADS):
         weight(c).wait()
     for c in range(2 * QUADS):
@@ -401,7 +398,7 @@
     )
     attend(items, before, after)
     projected(gh2_v, send2b_v)
-    for copy in third:
+    for copy in third[2:] + third[:2]:
         copy.start()
 
     for n in range(QUADS):

time: 36.4 us -> 35.9 us (0.986)
  Pallas kernels: 35.7 us -> 35.2 us
    pallas_call x1, Pallas kernels: 34.6 us -> 34.1 us  [shards(): pl.pallas_call(kernel, out_shape=[vmem((CELLS, WIDTH), bf16), vmem((CELLS...]
where the time goes in v5:
time: 35.9 us
  Pallas kernels  35.2 us (98%)
  between operations  0.66 us (2%)
    pallas_call x1, Pallas kernels, shards(): pl.pallas_call(kernel, out_shape=[vmem((CELLS, WIDTH), bf16), vmem((CELLS...  34.1 us
    pallas_call x1, Pallas kernels, shards(): pl.pallas_call(finish, out_shape=[jax.ShapeDtypeStruct((CELLS, WIDTH), bf...  1.07 us

profile of v5, /device:TPU:2, one launch (start us, length us, event | category | flops | bytes accessed | tf_op | source)
XLA Modules:
  0.0 35.9 jit_solution(11977798768122014481)
XLA Ops:
  0.6 0.0 copy-start
  0.6 34.1 %shard_map.77 = (bf16[256,1024]{1,0:T(8,128)(2,1)S(1)}, f32[256,1024]{1,0:T(8,128)S(1)}, f32[256,128]{1,0:T(8,128)S(1)}) custom-call(bf16[8,32,1024]{2,1,0:T(8,128)(2,1)} %x_hbm.1, bf16[256,1024]{1,0:T(8,128)(2,1)} %bitcast.6, f32[1,1024]{1,0:T(1,128)} %bitcast.7, s32[8,32]{1,0:T(8,128)} %corner_hbm.1, bf16[1024,3072]{1,0:T(8,128)(2,1)} %wqkv_hbm.1, ...), custom_call_target="tpu_custom_call" | custom-call | tf_op jit(solution)/shard_map/pallas_call | solution.py:460
  34.8 0.0 copy-done
  34.8 1.1 %shard_map.78 = (bf16[256,1024]{1,0:T(8,128)(2,1)}, bf16[256,1024]{1,0:T(8,128)(2,1)}) custom-call(bf16[256,1024]{1,0:T(8,128)(2,1)S(1)} %bitcast.5, bf16[256,1024]{1,0:T(8,128)(2,1)S(1)} %get-tuple-element.7.mixed_ref, f32[256,1024]{1,0:T(8,128)S(1)} %get-tuple-element.8.scaled_ref, f32[256,128]{1,0:T(8,128)S(1)} %get-tuple-element.9.inv_ref), custom_call_target="tpu_custom_call" | custom-call | tf_op jit(solution)/shard_map/pallas_call | solution.py:525
Async XLA Ops:
  0.6 34.2 %copy-start = (bf16[8,32,1024]{2,1,0:T(8,128)(2,1)S(1)}, bf16[8,32,1024]{2,1,0:T(8,128)(2,1)}, u32[]{:S(2)}) copy-start(bf16[8,32,1024]{2,1,0:T(8,128)(2,1)} %x_hbm.1) | copy-start | bytes 1572868

commit v6 on v5

--- a/solution.py
+++ b/solution.py
@@ -170,7 +170,10 @@
         weight(c).start()
     small[3].start()
     out_weight.start()
-    packt_v[...] = selection((CELLS, PACK), 1, 0)
+    places = lax.broadcasted_iota(jnp.int32, (PACK, PACK), 0)
+    outer = ((places & 63) >> 3) * COLS + (places & 7) + (COLS - TILE) * (places >> 6)
+    packed = piece_places(lax.broadcasted_iota(jnp.int32, (PACK, PACK), 1))[0]
+    packt_v[...] = jnp.where(packed == outer, 1.0, 0.0).astype(bf16)
     west_v[...] = selection((EDGE, SIDE), 1, 1)
     east_v[...] = selection((EDGE, SIDE), 1, 1, SIDE)
     spreadt_v[...] = selection((PACK, EDGE), 0, 1)
@@ -413,23 +416,32 @@
     g_v[:, :, pl.ds(0, WIDTH)] = gqf_v[...].astype(bf16)
     for n in range(QUADS):
         mixed_o[:, lanes(n)] = dot(att_v[...], wo_v[:, lanes(n)]).astype(bf16)
-        scaled_o[:, lanes(n)] += dot(
+        own = dot(
             g_v[:, :, pl.ds(0, WIDTH)].reshape(CELLS, WIDTH),
             w_v[lanes(n), pl.ds(0, WIDTH)],
             ROWS_BY_ROWS,
         )
-
-    for copy in second + third:
+        scaled_o[:, lanes(n)] = (scaled_o[:, lanes(n)] + own) * gain_v[:, lanes(n)]
+
+    def add_rims(ref, half):
+        for i, top in enumerate((0, ROWS - RADIUS)):
+            y = ref[n_s[i]].astype(f32) * gain
+            for r in range(RADIUS):
+                cells = pl.ds((top + r) * COLS + half * HALF, HALF)
+                scaled_o[cells] += y[r * HALF : (r + 1) * HALF]
+
+    for copy in second:
         copy.wait_recv()
-
-    def both(rows):
-        west, east = (r[rows].astype(f32).reshape(RADIUS, HALF, WIDTH) for r in (recv2a_r, recv2b_r))
-        return jnp.concatenate([west, east], axis=1).reshape(2 * RIM, WIDTH)
-
-    scaled_o[pl.ds(0, 2 * RIM)] += both(n_s[0])
-    scaled_o[pl.ds(CELLS - 2 * RIM, 2 * RIM)] += both(n_s[1])
-    edges = dot(packt_v[...], recv2b_r[pl.ds(2 * RIM, PACK)])
-    scaled_o[...] = (scaled_o[...] + edges) * gain
+    add_rims(recv2a_r, 0)
+    for copy in third:
+        copy.wait_recv()
+    add_rims(recv2b_r, 1)
+    edges = dot(packt_v[...], recv2b_r[pl.ds(2 * RIM, PACK)]) * gain
+    for side in range(2):
+        for r in range(ROWS):
+            cells = pl.ds(r * COLS + side * (COLS - TILE), TILE)
+            at = side * SIDE + r * TILE
+            scaled_o[cells] += edges[at : at + TILE]
     for copy in first[0] + first[1] + second + third:
         copy.wait_send()
 
@@ -474,7 +486,7 @@
             vmem((WIDTH, 3 * WIDTH), bf16),
             vmem((WIDTH, WIDTH), bf16),
             vmem((PACK, CELLS), bf16),
-            vmem((CELLS, PACK), bf16),
+            vmem((PACK, PACK), bf16),
             vmem((EDGE, SIDE), bf16),
             vmem((EDGE, SIDE), bf16),
             vmem((PACK, EDGE), bf16),

time: 35.9 us -> 36 us (level)
  no operation moved by 1% of the time
where the time goes in v6:
time: 36 us; the launch traced here: 35.9 us
  Pallas kernels  35.2 us (98%)
  between operations  0.66 us (2%)
    pallas_call x1, Pallas kernels, shards(): pl.pallas_call(kernel, out_shape=[vmem((CELLS, WIDTH), bf16), vmem((CELLS...  34.2 us
    pallas_call x1, Pallas kernels, shards(): pl.pallas_call(finish, out_shape=[jax.ShapeDtypeStruct((CELLS, WIDTH), bf...  1.07 us

profile of v6, /device:TPU:2, one launch (start us, length us, event | category | flops | bytes accessed | tf_op | source)
XLA Modules:
  0.0 35.9 jit_solution(11642027477010590059)
XLA Ops:
  0.6 0.0 copy-start
  0.6 34.2 %shard_map.77 = (bf16[256,1024]{1,0:T(8,128)(2,1)S(1)}, f32[256,1024]{1,0:T(8,128)S(1)}, f32[256,128]{1,0:T(8,128)S(1)}) custom-call(bf16[8,32,1024]{2,1,0:T(8,128)(2,1)} %x_hbm.1, bf16[256,1024]{1,0:T(8,128)(2,1)} %bitcast.6, f32[1,1024]{1,0:T(1,128)} %bitcast.7, s32[8,32]{1,0:T(8,128)} %corner_hbm.1, bf16[1024,3072]{1,0:T(8,128)(2,1)} %wqkv_hbm.1, ...), custom_call_target="tpu_custom_call" | custom-call | tf_op jit(solution)/shard_map/pallas_call | solution.py:472
  34.8 0.0 copy-done
  34.8 1.1 %shard_map.78 = (bf16[256,1024]{1,0:T(8,128)(2,1)}, bf16[256,1024]{1,0:T(8,128)(2,1)}) custom-call(bf16[256,1024]{1,0:T(8,128)(2,1)S(1)} %bitcast.5, bf16[256,1024]{1,0:T(8,128)(2,1)S(1)} %get-tuple-element.7.mixed_ref, f32[256,1024]{1,0:T(8,128)S(1)} %get-tuple-element.8.scaled_ref, f32[256,128]{1,0:T(8,128)S(1)} %get-tuple-element.9.inv_ref), custom_call_target="tpu_custom_call" | custom-call | tf_op jit(solution)/shard_map/pallas_call | solution.py:537
Async XLA Ops:
  0.6 34.2 %copy-start = (bf16[8,32,1024]{2,1,0:T(8,128)(2,1)S(1)}, bf16[8,32,1024]{2,1,0:T(8,128)(2,1)}, u32[]{:S(2)}) copy-start(bf16[8,32,1024]{2,1,0:T(8,128)(2,1)} %x_hbm.1) | copy-start | bytes 1572868
